TPU v7x, 32 devices: a whole 2x2x4 slice. The times are simulated.
32 devices in a mesh: replica: 8 (over z, x), group: 4 (over y, core).
Axes of the slice: x: 2, y: 2, z: 4, core: 2. Of those that a mesh axis runs over, the one named last changes fastest.
Arguments:
- inputs: bfloat16 [8192, 576], P(('replica', 'group')), may hold values from -6 to 6
- seg_ids: int32 [8192], P(('replica', 'group')), may hold values from 0 to 4, as said below
- seq_starts: int32 [6], replicated, may hold values from 0 to 8192, as said below
- gain_one: bfloat16 [576], P('group'), may hold values from 0.099609375 to 1.8984375
- query_w: bfloat16 [576, 576], P('group'), may hold values from -0.25 to 0.25
- key_w: bfloat16 [576, 192], P('group'), may hold values from -0.25 to 0.25
- value_weight: bfloat16 [576, 192], P('group'), may hold values from -0.25 to 0.25
- out_w: bfloat16 [576, 576], P('group'), may hold values from -2 to 2
- gain_two: bfloat16 [576], P('group'), may hold values from 0.099609375 to 1.8984375
- gate_w: bfloat16 [576, 1536], P('group'), may hold values from -0.25 to 0.25
- up_w: bfloat16 [576, 1536], P('group'), may hold values from -0.25 to 0.25
- down_w: bfloat16 [1536, 576], P('group'), may hold values from -0.15625 to 0.15625
- out_grad: bfloat16 [8192, 576], P(('replica', 'group')), may hold values from -6 to 6
Outputs:
- outputs: float32 [8192, 576], P(('replica', 'group'))
- grad_inputs: float32 [8192, 576], P(('replica', 'group'))
- grad_gain_one: float32 [576], P('group')
- grad_query_w: float32 [576, 576], P('group')
- grad_key_w: float32 [576, 192], P('group')
- grad_value_w: float32 [576, 192], P('group')
- grad_out_w: float32 [576, 576], P('group')
- grad_gain_two: float32 [576], P('group')
- grad_gate_w: float32 [576, 1536], P('group')
- grad_up_w: float32 [576, 1536], P('group')
- grad_down_w: float32 [1536, 576], P('group')
Inputs may be any that keep to these rules, and one draw needn't show every extreme that they name: seq_starts[0] is 0, seq_starts[1] lies between 1 and 2047, each later entry up to index 4 is 2048 more than the one before, and the last entry, at index 5, is 8192. seg_ids[i] is the number of entries of seq_starts after the first that are at most i; every sequence but the first and the last holds 2048 tokens.
All inputs are finite; a program needn't handle non-finite values.
Results may differ from a plain program's by a relative error of at most 0.017.
Values may be sent and summed in bfloat16 or wider, within the bound.
A program may use at most 128 MiB of HBM per device.

v0:
```python
import math

import jax
import jax.numpy as jnp
from jax import lax
from jax.sharding import PartitionSpec as P

HEAD_DIM = 64
SEQUENCE_LENGTH = 2048


epsilon = 1e-05
rope_base = 100000.0
masked_score = -1e30


def from_behind(block, axis, distance):
    devices = range(lax.axis_size(axis))
    route = [(i - distance, i) for i in devices if i - distance in devices]
    return lax.ppermute(block, axis, route)


def rms_scale(value_matrix):
    return lax.rsqrt(jnp.mean(value_matrix * value_matrix, axis=-1, keepdims=True) + epsilon)


def rope_angles(positions, head_size):
    frequency = jnp.exp(
        jnp.arange(0, head_size, 2, dtype=jnp.float32) * (-math.log(rope_base) / head_size)
    )
    return positions.astype(jnp.float32)[:, None] * frequency[None, :]


def apply_rotary(value_matrix, rotary_angles):
    middle_cut = value_matrix.shape[-1] // 2
    former = value_matrix[..., :middle_cut]
    latter = value_matrix[..., middle_cut:]
    cosine = jnp.cos(rotary_angles)[:, None, :]
    sine_part = jnp.sin(rotary_angles)[:, None, :]
    return jnp.concatenate(
        [former * cosine - latter * sine_part, latter * cosine + former * sine_part], axis=-1
    )


def contract_rows(former, latter):
    return lax.dot_general(
        former, latter, (((0,), (0,)), ((), ())), preferred_element_type=jnp.float32
    )


def times_transpose(former, latter):
    return lax.dot_general(
        former, latter, (((1,), (1,)), ((), ())), preferred_element_type=jnp.float32
    )


def norm_back(grad_normed, value_matrix, scale_rows, gain_wide):
    weighted = grad_normed * gain_wide
    cubed = scale_rows * scale_rows * scale_rows
    grad_values = scale_rows * weighted - value_matrix * cubed * jnp.mean(
        weighted * value_matrix, axis=-1, keepdims=True
    )
    grad_gain = jnp.sum(grad_normed * value_matrix * scale_rows, axis=0)
    return (grad_values, grad_gain)


def per_device(
    inputs,
    seg_ids,
    seq_starts,
    gain_one,
    query_w,
    key_w,
    value_weight,
    out_w,
    gain_two,
    gate_w,
    up_w,
    down_w,
    out_grad,
):
    (
        gain_one_all,
        query_all,
        key_all,
        value_all,
        out_all,
        gain_two_all,
        gate_all,
        up_all,
        down_all,
    ) = (
        lax.all_gather(gain_one, "group", axis=0, tiled=True),
        lax.all_gather(query_w, "group", axis=0, tiled=True),
        lax.all_gather(key_w, "group", axis=0, tiled=True),
        lax.all_gather(value_weight, "group", axis=0, tiled=True),
        lax.all_gather(out_w, "group", axis=0, tiled=True),
        lax.all_gather(gain_two, "group", axis=0, tiled=True),
        lax.all_gather(gate_w, "group", axis=0, tiled=True),
        lax.all_gather(up_w, "group", axis=0, tiled=True),
        lax.all_gather(down_w, "group", axis=0, tiled=True),
    )
    tok_rows = inputs.shape[0]
    query_heads = query_all.shape[1] // HEAD_DIM
    kv_heads = key_all.shape[1] // HEAD_DIM
    repeat_heads = query_heads // kv_heads
    kv_width = kv_heads * HEAD_DIM
    score_scale = 1.0 / math.sqrt(HEAD_DIM)
    reach_back = SEQUENCE_LENGTH // tok_rows
    window_rows = (reach_back + 1) * tok_rows
    device = lax.axis_index(("replica", "group"))
    token_index = device * tok_rows + jnp.arange(tok_rows, dtype=jnp.int32)
    segment_table = jnp.arange(seq_starts.shape[0], dtype=jnp.int32)
    first_token = jnp.sum(
        jnp.where(seg_ids[:, None] == segment_table[None, :], seq_starts[None, :], 0), axis=1
    )
    rotary_angles = rope_angles(token_index - first_token, HEAD_DIM)
    key_index = (device - reach_back) * tok_rows + jnp.arange(window_rows, dtype=jnp.int32)
    visible = (key_index[None, :] <= token_index[:, None]) & (
        key_index[None, :] >= first_token[:, None]
    )
    inputs_wide = inputs.astype(jnp.float32)
    scale_one = rms_scale(inputs_wide)
    gain_one_wide = gain_one_all.astype(jnp.float32)
    first_normed = (inputs_wide * scale_one * gain_one_wide).astype(jnp.bfloat16)
    joined_w = jnp.concatenate([query_all, key_all, value_all], axis=1)
    projected = jnp.dot(first_normed, joined_w, preferred_element_type=jnp.float32)
    query_cols = query_heads * HEAD_DIM
    queries = apply_rotary(
        projected[:, :query_cols].reshape(tok_rows, query_heads, HEAD_DIM), rotary_angles
    ).astype(jnp.bfloat16)
    key_matrix = apply_rotary(
        projected[:, query_cols : query_cols + kv_width].reshape(tok_rows, kv_heads, HEAD_DIM),
        rotary_angles,
    )
    key_matrix = key_matrix.astype(jnp.bfloat16).reshape(tok_rows, kv_width)
    value_matrix = projected[:, query_cols + kv_width :].astype(jnp.bfloat16)
    packed = jnp.concatenate([key_matrix, value_matrix], axis=1)
    blocks = [packed]
    for offset in range(1, reach_back + 1):
        blocks.insert(0, from_behind(packed, ("replica", "group"), offset))
    window = jnp.concatenate(blocks, axis=0)
    key_grid = window[:, :kv_width].reshape(window_rows, kv_heads, HEAD_DIM)
    value_grid = window[:, kv_width:].reshape(window_rows, kv_heads, HEAD_DIM)
    query_grid = queries.reshape(tok_rows, kv_heads, repeat_heads, HEAD_DIM)

    def masked_scores():
        raw_scores = (
            jnp.einsum("tcrd,wcd->crtw", query_grid, key_grid, preferred_element_type=jnp.float32)
            * score_scale
        )
        return jnp.where(visible, raw_scores, masked_score)

    scores = masked_scores()
    row_peak = jnp.max(scores, axis=-1, keepdims=True)
    exponent = jnp.exp(scores - row_peak)
    row_total = jnp.sum(exponent, axis=-1, keepdims=True)
    log_total = row_peak + jnp.log(row_total)
    probs_low = (exponent / row_total).astype(jnp.bfloat16)
    attended = jnp.einsum(
        "crtw,wcd->tcrd", probs_low, value_grid, preferred_element_type=jnp.float32
    )
    attended = attended.reshape(tok_rows, query_cols).astype(jnp.bfloat16)
    middle = inputs_wide + jnp.dot(attended, out_all, preferred_element_type=jnp.float32)
    scale_two = rms_scale(middle)
    gain_two_wide = gain_two_all.astype(jnp.float32)
    normed_two = (middle * scale_two * gain_two_wide).astype(jnp.bfloat16)
    gate = jnp.dot(normed_two, gate_all, preferred_element_type=jnp.float32)
    upper = jnp.dot(normed_two, up_all, preferred_element_type=jnp.float32)
    sigmoid_gate = jax.nn.sigmoid(gate)
    hidden = (gate * sigmoid_gate * upper).astype(jnp.bfloat16)
    outputs = middle + jnp.dot(hidden, down_all, preferred_element_type=jnp.float32)
    grad_hidden = times_transpose(out_grad, down_all)
    grad_gate = (grad_hidden * upper * sigmoid_gate * (1.0 + gate * (1.0 - sigmoid_gate))).astype(
        jnp.bfloat16
    )
    grad_up = (grad_hidden * gate * sigmoid_gate).astype(jnp.bfloat16)
    grad_normed_two = times_transpose(grad_gate, gate_all) + times_transpose(grad_up, up_all)
    grad_middle_norm, grad_gain_two = norm_back(grad_normed_two, middle, scale_two, gain_two_wide)
    grad_middle = out_grad.astype(jnp.float32) + grad_middle_norm
    grad_branch = grad_middle.astype(jnp.bfloat16)
    grad_attended = (
        times_transpose(grad_branch, out_all)
        .astype(jnp.bfloat16)
        .reshape(tok_rows, kv_heads, repeat_heads, HEAD_DIM)
    )
    scores_again = masked_scores()
    probs = jnp.exp(scores_again - log_total)
    probs_again = probs.astype(jnp.bfloat16)
    grad_probs = jnp.einsum(
        "tcrd,wcd->crtw", grad_attended, value_grid, preferred_element_type=jnp.float32
    )
    inner = jnp.sum(probs * grad_probs, axis=-1, keepdims=True)
    grad_scores = (probs * (grad_probs - inner)).astype(jnp.bfloat16)
    grad_query_rot = (
        jnp.einsum("crtw,wcd->tcrd", grad_scores, key_grid, preferred_element_type=jnp.float32)
        * score_scale
    )
    grad_key_rot = (
        jnp.einsum("crtw,tcrd->wcd", grad_scores, query_grid, preferred_element_type=jnp.float32)
        * score_scale
    )
    grad_value_win = jnp.einsum(
        "crtw,tcrd->wcd", probs_again, grad_attended, preferred_element_type=jnp.float32
    )
    grad_window = jnp.concatenate(
        [
            grad_key_rot.reshape(window_rows, kv_width),
            grad_value_win.reshape(window_rows, kv_width),
        ],
        axis=1,
    )
    own_grad = grad_window[reach_back * tok_rows :]
    for offset in range(1, reach_back + 1):
        lower_edge = (reach_back - offset) * tok_rows
        own_grad = own_grad + from_behind(
            grad_window[lower_edge : lower_edge + tok_rows].astype(jnp.bfloat16),
            ("replica", "group"),
            -offset,
        ).astype(jnp.float32)
    grad_keys = apply_rotary(
        own_grad[:, :kv_width].reshape(tok_rows, kv_heads, HEAD_DIM), -rotary_angles
    )
    grad_keys = grad_keys.reshape(tok_rows, kv_width).astype(jnp.bfloat16)
    grad_values = own_grad[:, kv_width:].astype(jnp.bfloat16)
    grad_queries = apply_rotary(
        grad_query_rot.reshape(tok_rows, query_heads, HEAD_DIM), -rotary_angles
    )
    grad_queries = grad_queries.reshape(tok_rows, query_cols).astype(jnp.bfloat16)
    grad_normed_one = (
        times_transpose(grad_queries, query_all)
        + times_transpose(grad_keys, key_all)
        + times_transpose(grad_values, value_all)
    )
    grad_inputs_norm, grad_gain_one = norm_back(
        grad_normed_one, inputs_wide, scale_one, gain_one_wide
    )
    grad_inputs = grad_middle + grad_inputs_norm
    grad_query_w = contract_rows(first_normed, grad_queries)
    grad_key_w = contract_rows(first_normed, grad_keys)
    grad_value_w = contract_rows(first_normed, grad_values)
    grad_out_w = contract_rows(attended, grad_branch)
    grad_gate_w = contract_rows(normed_two, grad_gate)
    grad_up_w = contract_rows(normed_two, grad_up)
    grad_down_w = contract_rows(hidden, out_grad)
    owner_sums = (
        lax.psum_scatter(
            grad_gain_one.astype(jnp.bfloat16), "group", scatter_dimension=0, tiled=True
        ).astype(jnp.float32),
        lax.psum_scatter(
            grad_query_w.astype(jnp.bfloat16), "group", scatter_dimension=0, tiled=True
        ).astype(jnp.float32),
        lax.psum_scatter(
            grad_key_w.astype(jnp.bfloat16), "group", scatter_dimension=0, tiled=True
        ).astype(jnp.float32),
        lax.psum_scatter(
            grad_value_w.astype(jnp.bfloat16), "group", scatter_dimension=0, tiled=True
        ).astype(jnp.float32),
        lax.psum_scatter(
            grad_out_w.astype(jnp.bfloat16), "group", scatter_dimension=0, tiled=True
        ).astype(jnp.float32),
        lax.psum_scatter(
            grad_gain_two.astype(jnp.bfloat16), "group", scatter_dimension=0, tiled=True
        ).astype(jnp.float32),
        lax.psum_scatter(
            grad_gate_w.astype(jnp.bfloat16), "group", scatter_dimension=0, tiled=True
        ).astype(jnp.float32),
        lax.psum_scatter(
            grad_up_w.astype(jnp.bfloat16), "group", scatter_dimension=0, tiled=True
        ).astype(jnp.float32),
        lax.psum_scatter(
            grad_down_w.astype(jnp.bfloat16), "group", scatter_dimension=0, tiled=True
        ).astype(jnp.float32),
    )
    totals = lax.psum(
        (
            owner_sums[0],
            owner_sums[1],
            owner_sums[2],
            owner_sums[3],
            owner_sums[4],
            owner_sums[5],
            owner_sums[6],
            owner_sums[7],
            owner_sums[8],
        ),
        "replica",
    )
    return (
        outputs,
        grad_inputs,
        totals[0],
        totals[1],
        totals[2],
        totals[3],
        totals[4],
        totals[5],
        totals[6],
        totals[7],
        totals[8],
    )


def solution(mesh):
    placed = (
        P(("replica", "group"), None),
        P(("replica", "group")),
        P(),
        P("group"),
        P("group", None),
        P("group", None),
        P("group", None),
        P("group", None),
        P("group"),
        P("group", None),
        P("group", None),
        P("group", None),
        P(("replica", "group"), None),
    )
    return jax.shard_map(
        per_device,
        mesh=mesh,
        in_specs=placed,
        out_specs=(
            P(("replica", "group"), None),
            P(("replica", "group"), None),
            P("group"),
            P("group", None),
            P("group", None),
            P("group", None),
            P("group", None),
            P("group"),
            P("group", None),
            P("group", None),
            P("group", None),
        ),
        check_vma=False,
    )
```

profile of v0, /device:TPU:0, one launch (start us, length us, event | category | flops | bytes accessed | tf_op | source)
XLA Modules:
  0.0 555.4 jit_solution(8550212888770973284)
XLA Ops:
  12.5 8.3 %all-reduce.6 = (bf16[576]{0:T(1024)(128)(2,1)S(1)}, bf16[576]{0:T(1024)(128)(2,1)S(1)}) all-reduce(bf16[576]{0:T(1024)(128)(2,1)S(1)} %dynamic-update-slice, bf16[576]{0:T(1024)(128)(2,1)S(1)} %dynamic-update-slice.1), channel_id=1, replica_groups=mesh['replica'=8,'group'=4] {'group'}, use_global_device_ids=true, to_apply=%add | all-reduce | flops 1152 | bytes 4608
  20.8 7.7 %all_gather.30 = bf16[576,192]{1,0:T(8,128)(2,1)S(1)} all-gather(bf16[144,192]{1,0:T(8,128)(2,1)} %param.19), channel_id=1, replica_groups=mesh['replica'=8,'group'=4] {'group'}, dimensions={0}, use_global_device_ids=true | all-gather | bytes 276480 | tf_op jit(solution)/shard_map/all_gather | solution.py:96
  28.6 7.0 %all_gather.29 = bf16[576,192]{1,0:T(8,128)(2,1)S(1)} all-gather(bf16[144,192]{1,0:T(8,128)(2,1)} %param.18), channel_id=1, replica_groups=mesh['replica'=8,'group'=4] {'group'}, dimensions={0}, use_global_device_ids=true | all-gather | bytes 276480 | tf_op jit(solution)/shard_map/all_gather | solution.py:95
  36.3 8.5 %all_gather.28 = bf16[576,576]{1,0:T(8,128)(2,1)S(1)} all-gather(bf16[144,576]{1,0:T(8,128)(2,1)S(1)} %copy-done.38), channel_id=1, replica_groups=mesh['replica'=8,'group'=4] {'group'}, dimensions={0}, use_global_device_ids=true | all-gather | bytes 829440 | tf_op jit(solution)/shard_map/all_gather | solution.py:94
  46.9 3.4 collective-permute-start
  53.4 4.3 collective-permute-start.2
  59.9 3.4 collective-permute-start.4
  63.5 9.1 %all_gather.31 = bf16[576,576]{1,0:T(8,128)(2,1)S(1)} all-gather(bf16[144,576]{1,0:T(8,128)(2,1)S(1)} %copy-done.39), channel_id=1, replica_groups=mesh['replica'=8,'group'=4] {'group'}, dimensions={0}, use_global_device_ids=true | all-gather | bytes 829440 | tf_op jit(solution)/shard_map/all_gather | solution.py:97
  76.0 3.4 collective-permute-start.6
  84.1 8.4 %collective-permute-done.6 = bf16[256,384]{0,1:T(8,128)(2,1)S(1)} collective-permute-done((bf16[256,384]{0,1:T(8,128)(2,1)S(1)}, bf16[256,384]{0,1:T(8,128)(2,1)S(1)}, u32[]{:S(2)}, u32[]{:S(2)}) %collective-permute-start.6) | collective-permute-done | bytes 196640 | tf_op jit(solution)/shard_map/ppermute | solution.py:20
  92.7 3.3 fusion.50
  96.0 3.1 fusion.3
  99.2 3.9 copy-done
  103.1 3.9 fusion.11
  108.3 3.4 fusion.51
  111.8 3.5 fusion.52
  115.2 4.8 multiply_convert_fusion
  125.0 13.2 %fusion = (f32[3,3,256]{2,1,0:T(4,128)S(1)}, f32[3,2304,256,3]{2,1,3,0:T(8,128)}) fusion(f32[3,3,256,2304]{2,3,1,0:T(8,128)} %copy-done, f32[3,3,256]{2,1,0:T(4,128)S(1)} %log_add_fusion, bf16[2304,3,64,1]{0,2,3,1:T(8,128)(2,1)S(1)} %bitcast.97, bf16[256,3,3,64]{0,3,2,1:T(8,128)(2,1)S(1)} %bitcast.100), kind=kOutput, calls=%fused_computation.2 | convolution fusion | flops 695400192 | bytes 43665408 | tf_op jit(solution)/shard_map/tcrd,wcd->crtw/dot_general | solution.py:190
  138.2 8.8 %fusion.5 = f32[3,64,2304,1]{2,1,3,0:T(8,128)S(1)} fusion(bf16[256,3,3,64]{0,3,2,1:T(8,128)(2,1)S(1)} %bitcast.101, f32[3,3,256,2304]{2,3,1,0:T(8,128)} %copy-done, f32[3,3,256]{2,1,0:T(4,128)S(1)} %log_add_fusion), kind=kOutput, calls=%fused_computation.11 | convolution fusion | flops 690094080 | bytes 23307264 | tf_op jit(solution)/shard_map/crtw,tcrd->wcd/dot_general | solution.py:203
  147.1 14.5 %fusion.2 = bf16[3,3,256,2304]{2,3,1,0:T(8,128)(2,1)S(1)} fusion(f32[3,2304,256,3]{2,1,3,0:T(8,128)} %get-tuple-element.65, f32[3,3,256,2304]{2,3,1,0:T(8,128)} %copy-done, f32[3,3,256]{2,1,0:T(4,128)S(1)} %get-tuple-element.64, f32[3,3,256]{2,1,0:T(4,128)S(1)} %log_add_fusion), kind=kLoop, calls=%fused_computation.4 | loop fusion | flops 21233664 | bytes 53102592 | tf_op jit(solution)/shard_map/convert_element_type | solution.py:194
  161.6 3.3 fusion.9
  172.5 3.9 collective-permute-done.15
  185.4 4.2 collective-permute-done.9
  191.7 6.8 %convolution_multiply_fusion = f32[3,64,3,256]{3,1,2,0:T(8,128)} fusion(bf16[2304,3,64,1]{0,2,3,1:T(8,128)(2,1)S(1)} %bitcast.95, bf16[3,3,256,2304]{2,3,1,0:T(8,128)(2,1)} %copy-done.1), kind=kOutput, calls=%fused_computation.37 | convolution fusion | flops 679624704 | bytes 12091392 | tf_op jit(solution)/shard_map/crtw,wcd->tcrd/dot_general | solution.py:196
  218.7 12.5 %all-reduce.5 = (bf16[576]{0:T(1024)(128)(2,1)S(1)}, bf16[576]{0:T(1024)(128)(2,1)S(1)}) all-reduce(bf16[576]{0:T(1024)(128)(2,1)S(1)} %get-tuple-element.13, bf16[576]{0:T(1024)(128)(2,1)S(1)} %copy-done.46), channel_id=2, replica_groups=mesh['replica'=8,'group'=4] {'group'}, use_global_device_ids=true, to_apply=%region_9.10.clone | all-reduce | flops 1152 | bytes 4608
  232.3 16.7 %reduce-scatter.14.cloned.1.call-done = bf16[144,192]{1,0:T(8,128)(2,1)} async-done(((bf16[576,192]{1,0:T(8,128)(2,1)}), bf16[144,192]{1,0:T(8,128)(2,1)}) %reduce-scatter.14.cloned.1.call-update) | async-done | bytes 55312 | tf_op jit(solution)/shard_map/reduce_scatter | solution.py:256
  249.1 26.0 %reduce-scatter.10.cloned.1.call-done = bf16[144,576]{1,0:T(8,128)(2,1)} async-done(((bf16[576,576]{1,0:T(8,128)(2,1)}), bf16[144,576]{1,0:T(8,128)(2,1)}) %reduce-scatter.10.cloned.1.call-update) | async-done | bytes 165904 | tf_op jit(solution)/shard_map/reduce_scatter | solution.py:250
  275.0 26.3 %reduce-scatter.16.cloned.1.call-done = bf16[144,576]{1,0:T(8,128)(2,1)} async-done(((bf16[576,576]{1,0:T(8,128)(2,1)}), bf16[144,576]{1,0:T(8,128)(2,1)}) %reduce-scatter.16.cloned.1.call-update) | async-done | bytes 165904 | tf_op jit(solution)/shard_map/reduce_scatter | solution.py:259
  301.3 33.2 %reduce-scatter.22.cloned.1.call-done = bf16[384,576]{1,0:T(8,128)(2,1)} async-done(((bf16[1536,576]{1,0:T(8,128)(2,1)}), bf16[384,576]{1,0:T(8,128)(2,1)}) %reduce-scatter.22.cloned.1.call-update) | async-done | bytes 442384
  335.8 30.9 %reduce-scatter.18.cloned.1.call-done = bf16[144,1536]{1,0:T(8,128)(2,1)} async-done(((bf16[576,1536]{1,0:T(8,128)(2,1)}), bf16[144,1536]{1,0:T(8,128)(2,1)}) %reduce-scatter.18.cloned.1.call-update) | async-done | bytes 442384 | tf_op jit(solution)/shard_map/reduce_scatter | solution.py:265
  366.7 31.8 %reduce-scatter.20.cloned.1.call-done = bf16[144,1536]{1,0:T(8,128)(2,1)} async-done(((bf16[576,1536]{1,0:T(8,128)(2,1)}), bf16[144,1536]{1,0:T(8,128)(2,1)}) %reduce-scatter.20.cloned.1.call-update) | async-done | bytes 442384 | tf_op jit(solution)/shard_map/reduce_scatter | solution.py:268
  398.6 149.9 %all-reduce.8 = (f32[144]{0:T(256)}, f32[144,576]{1,0:T(8,128)}, f32[144,192]{1,0:T(8,128)}, f32[144,192]{1,0:T(8,128)}, f32[144,576]{1,0:T(8,128)}, /*index=5*/...) all-reduce(f32[144]{0:T(256)S(1)} %dynamic-slice_convert_fusion.1, ...), channel_id=1, replica_groups=mesh['replica'=8,'group'=4] {'replica'}, use_global_device_ids=true, to_apply=%region_10.11 | all-reduce | flops 885024 | bytes 5310720 | tf_op jit(solution)/shard_map/psum | solution.py:275
  (217 shorter events, 67.2 us)
Async XLA Ops:
  7.2 28.4 %copy-start.2 = (bf16[256,576]{0,1:T(8,128)(2,1)S(1)}, bf16[256,576]{0,1:T(8,128)(2,1)}, u32[]{:S(2)}) copy-start(bf16[256,576]{0,1:T(8,128)(2,1)} %param.13) | copy-start | bytes 884740
  7.2 29.1 %copy-start.38 = (bf16[144,576]{1,0:T(8,128)(2,1)S(1)}, bf16[144,576]{1,0:T(8,128)(2,1)}, u32[]{:S(2)}) copy-start(bf16[144,576]{1,0:T(8,128)(2,1)} %param.17) | copy-start | bytes 497668
  7.2 101.1 %all-gather.4.cloned.1.call-start = ((), (), s32[]{:S(2)}) async-start(), calls=%async_computation.7 | async-start | bytes 2211840 | tf_op jit(solution)/shard_map/all_gather | solution.py:99
  7.9 103.8 %all-gather.6.cloned.1.call-start = ((), (), s32[]{:S(2)}) async-start(), calls=%async_computation.8 | async-start | bytes 2211840 | tf_op jit(solution)/shard_map/all_gather | solution.py:100
  8.7 106.6 %all-gather.8.cloned.1.call-start = ((), (), s32[]{:S(2)}) async-start(), calls=%async_computation.9 | async-start | bytes 2211840 | tf_op jit(solution)/shard_map/all_gather | solution.py:101
  46.9 26.8 %collective-permute-start = (bf16[256,384]{0,1:T(8,128)(2,1)S(1)}, bf16[256,384]{0,1:T(8,128)(2,1)S(1)}, u32[]{:S(2)}, u32[]{:S(2)}) collective-permute-start(bf16[256,384]{0,1:T(8,128)(2,1)S(1)} %pad_maximum_fusion.3), channel_id=1, source_target_pairs={{0,8},{1,9},{2,10},{3,11},{4,12},{5,13},{6,14},{7,15},{8,16},{9,17... | collective-permute-start | bytes 589832 | tf_op jit(solution)/shard_map/ppermute | solution.py:20
  50.3 25.6 %collective-permute-start.1 = (bf16[256,384]{0,1:T(8,128)(2,1)S(1)}, bf16[256,384]{0,1:T(8,128)(2,1)S(1)}, u32[]{:S(2)}, u32[]{:S(2)}) collective-permute-start(bf16[256,384]{0,1:T(8,128)(2,1)S(1)} %pad_maximum_fusion.3), channel_id=1, source_target_pairs={{0,7},{1,8},{2,9},{3,10},{4,11},{5,12},{6,13},{7,14},{8,15},{9,16}... | collective-permute-start | bytes 589832 | tf_op jit(solution)/shard_map/ppermute | solution.py:20
  53.4 26.1 %collective-permute-start.2 = (bf16[256,384]{0,1:T(8,128)(2,1)S(1)}, bf16[256,384]{0,1:T(8,128)(2,1)S(1)}, u32[]{:S(2)}, u32[]{:S(2)}) collective-permute-start(bf16[256,384]{0,1:T(8,128)(2,1)S(1)} %pad_maximum_fusion.3), channel_id=1, source_target_pairs={{0,6},{1,7},{2,8},{3,9},{4,10},{5,11},{6,12},{7,13},{8,14},{9,15},... | collective-permute-start | bytes 589832 | tf_op jit(solution)/shard_map/ppermute | solution.py:20
  57.7 23.4 %collective-permute-start.3 = (bf16[256,384]{0,1:T(8,128)(2,1)S(1)}, bf16[256,384]{0,1:T(8,128)(2,1)S(1)}, u32[]{:S(2)}, u32[]{:S(2)}) collective-permute-start(bf16[256,384]{0,1:T(8,128)(2,1)S(1)} %pad_maximum_fusion.3), channel_id=1, source_target_pairs={{0,5},{1,6},{2,7},{3,8},{4,9},{5,10},{6,11},{7,12},{8,13},{9,14},{... | collective-permute-start | bytes 589832 | tf_op jit(solution)/shard_map/ppermute | solution.py:20
  59.9 21.2 %collective-permute-start.4 = (bf16[256,384]{0,1:T(8,128)(2,1)S(1)}, bf16[256,384]{0,1:T(8,128)(2,1)S(1)}, u32[]{:S(2)}, u32[]{:S(2)}) collective-permute-start(bf16[256,384]{0,1:T(8,128)(2,1)S(1)} %pad_maximum_fusion.3), channel_id=1, source_target_pairs={{0,4},{1,5},{2,6},{3,7},{4,8},{5,9},{6,10},{7,11},{8,12},{9,13},{1... | collective-permute-start | bytes 589832 | tf_op jit(solution)/shard_map/ppermute | solution.py:20
  63.4 168.9 %reduce-scatter.12.cloned.1.call-start = ((), (), s32[]{:S(2)}) async-start(), calls=%async_computation.11 | async-start | bytes 368640 | tf_op jit(solution)/shard_map/reduce_scatter | solution.py:253
  72.5 34.5 %copy-start.5 = (bf16[576,576]{1,0:T(8,128)(2,1)}, bf16[576,576]{1,0:T(8,128)(2,1)S(1)}, u32[]{:S(2)}) copy-start(bf16[576,576]{1,0:T(8,128)(2,1)S(1)} %all_gather.31) | copy-start | bytes 1990660
  73.7 19.0 %copy-start.30 = (bf16[256,9,32]{0,2,1:T(8,128)(2,1)}, bf16[256,9,32]{0,2,1:T(8,128)(2,1)S(1)}, u32[]{:S(2)}) copy-start(bf16[256,9,32]{0,2,1:T(8,128)(2,1)S(1)} %get-tuple-element.43) | copy-start | bytes 442372
  73.7 19.0 %copy-start.32 = (bf16[256,9,32]{0,2,1:T(8,128)(2,1)}, bf16[256,9,32]{0,2,1:T(8,128)(2,1)S(1)}, u32[]{:S(2)}) copy-start(bf16[256,9,32]{0,2,1:T(8,128)(2,1)S(1)} %get-tuple-element.44) | copy-start | bytes 442372
  73.8 34.4 %copy-start.40 = (f32[576]{0:T(1024)}, f32[576]{0:T(1024)S(1)}, u32[]{:S(2)}) copy-start(f32[576]{0:T(1024)S(1)} %convert_element_type.170) | copy-start | bytes 6916
  73.8 10.3 %collective-permute-start.5 = (bf16[256,384]{0,1:T(8,128)(2,1)S(1)}, bf16[256,384]{0,1:T(8,128)(2,1)S(1)}, u32[]{:S(2)}, u32[]{:S(2)}) collective-permute-start(bf16[256,384]{0,1:T(8,128)(2,1)S(1)} %pad_maximum_fusion.3), channel_id=1, source_target_pairs={{0,3},{1,4},{2,5},{3,6},{4,7},{5,8},{6,9},{7,10},{8,11},{9,12},{10... | collective-permute-start | bytes 589832 | tf_op jit(solution)/shard_map/ppermute | solution.py:20
  76.0 16.5 %collective-permute-start.6 = (bf16[256,384]{0,1:T(8,128)(2,1)S(1)}, bf16[256,384]{0,1:T(8,128)(2,1)S(1)}, u32[]{:S(2)}, u32[]{:S(2)}) collective-permute-start(bf16[256,384]{0,1:T(8,128)(2,1)S(1)} %pad_maximum_fusion.3), channel_id=1, source_target_pairs={{0,2},{1,3},{2,4},{3,5},{4,6},{5,7},{6,8},{7,9},{8,10},{9,11},{10,... | collective-permute-start | bytes 589832 | tf_op jit(solution)/shard_map/ppermute | solution.py:20
  79.4 13.1 %collective-permute-start.7 = (bf16[256,384]{0,1:T(8,128)(2,1)S(1)}, bf16[256,384]{0,1:T(8,128)(2,1)S(1)}, u32[]{:S(2)}, u32[]{:S(2)}) collective-permute-start(bf16[256,384]{0,1:T(8,128)(2,1)S(1)} %pad_maximum_fusion.3), channel_id=1, source_target_pairs={{0,1},{1,2},{2,3},{3,4},{4,5},{5,6},{6,7},{7,8},{8,9},{9,10},{10,1... | collective-permute-start | bytes 589832 | tf_op jit(solution)/shard_map/ppermute | solution.py:20
  166.0 10.4 %collective-permute-start.15 = (bf16[256,384]{0,1:T(8,128)(2,1)S(1)}, bf16[256,384]{0,1:T(8,128)(2,1)S(1)}, u32[]{:S(2)}, u32[]{:S(2)}) collective-permute-start(bf16[256,384]{0,1:T(8,128)(2,1)S(1)} %get-tuple-element.32), channel_id=1, source_target_pairs={{8,0},{9,1},{10,2},{11,3},{12,4},{13,5},{14,6},{15,7},{16,8},{17,9... | collective-permute-start | bytes 589832 | tf_op jit(solution)/shard_map/ppermute | solution.py:20
  167.3 10.4 %collective-permute-start.14 = (bf16[256,384]{0,1:T(8,128)(2,1)S(1)}, bf16[256,384]{0,1:T(8,128)(2,1)S(1)}, u32[]{:S(2)}, u32[]{:S(2)}) collective-permute-start(bf16[256,384]{0,1:T(8,128)(2,1)S(1)} %get-tuple-element.33), channel_id=1, source_target_pairs={{7,0},{8,1},{9,2},{10,3},{11,4},{12,5},{13,6},{14,7},{15,8},{16,9}... | collective-permute-start | bytes 589832 | tf_op jit(solution)/shard_map/ppermute | solution.py:20
  168.6 13.2 %collective-permute-start.13 = (bf16[256,384]{0,1:T(8,128)(2,1)S(1)}, bf16[256,384]{0,1:T(8,128)(2,1)S(1)}, u32[]{:S(2)}, u32[]{:S(2)}) collective-permute-start(bf16[256,384]{0,1:T(8,128)(2,1)S(1)} %get-tuple-element.34), channel_id=1, source_target_pairs={{6,0},{7,1},{8,2},{9,3},{10,4},{11,5},{12,6},{13,7},{14,8},{15,9},... | collective-permute-start | bytes 589832 | tf_op jit(solution)/shard_map/ppermute | solution.py:20
  169.9 13.4 %collective-permute-start.12 = (bf16[256,384]{0,1:T(8,128)(2,1)S(1)}, bf16[256,384]{0,1:T(8,128)(2,1)S(1)}, u32[]{:S(2)}, u32[]{:S(2)}) collective-permute-start(bf16[256,384]{0,1:T(8,128)(2,1)S(1)} %get-tuple-element.35), channel_id=1, source_target_pairs={{5,0},{6,1},{7,2},{8,3},{9,4},{10,5},{11,6},{12,7},{13,8},{14,9},{... | collective-permute-start | bytes 589832 | tf_op jit(solution)/shard_map/ppermute | solution.py:20
  171.2 12.1 %collective-permute-start.11 = (bf16[256,384]{0,1:T(8,128)(2,1)S(1)}, bf16[256,384]{0,1:T(8,128)(2,1)S(1)}, u32[]{:S(2)}, u32[]{:S(2)}) collective-permute-start(bf16[256,384]{0,1:T(8,128)(2,1)S(1)} %get-tuple-element.36), channel_id=1, source_target_pairs={{4,0},{5,1},{6,2},{7,3},{8,4},{9,5},{10,6},{11,7},{12,8},{13,9},{1... | collective-permute-start | bytes 589832 | tf_op jit(solution)/shard_map/ppermute | solution.py:20
  176.4 9.1 %collective-permute-start.10 = (bf16[256,384]{0,1:T(8,128)(2,1)S(1)}, bf16[256,384]{0,1:T(8,128)(2,1)S(1)}, u32[]{:S(2)}, u32[]{:S(2)}) collective-permute-start(bf16[256,384]{0,1:T(8,128)(2,1)S(1)} %get-tuple-element.37), channel_id=1, source_target_pairs={{3,0},{4,1},{5,2},{6,3},{7,4},{8,5},{9,6},{10,7},{11,8},{12,9},{13... | collective-permute-start | bytes 589832 | tf_op jit(solution)/shard_map/ppermute | solution.py:20
  177.7 11.9 %collective-permute-start.9 = (bf16[256,384]{0,1:T(8,128)(2,1)S(1)}, bf16[256,384]{0,1:T(8,128)(2,1)S(1)}, u32[]{:S(2)}, u32[]{:S(2)}) collective-permute-start(bf16[256,384]{0,1:T(8,128)(2,1)S(1)} %get-tuple-element.38), channel_id=1, source_target_pairs={{2,0},{3,1},{4,2},{5,3},{6,4},{7,5},{8,6},{9,7},{10,8},{11,9},{12,... | collective-permute-start | bytes 589832 | tf_op jit(solution)/shard_map/ppermute | solution.py:20
  181.8 7.8 %collective-permute-start.8 = (bf16[256,384]{0,1:T(8,128)(2,1)S(1)}, bf16[256,384]{0,1:T(8,128)(2,1)S(1)}, u32[]{:S(2)}, u32[]{:S(2)}) collective-permute-start(bf16[256,384]{0,1:T(8,128)(2,1)S(1)} %get-tuple-element.31), channel_id=1, source_target_pairs={{1,0},{2,1},{3,2},{4,3},{5,4},{6,5},{7,6},{8,7},{9,8},{10,9},{11,1... | collective-permute-start | bytes 589832 | tf_op jit(solution)/shard_map/ppermute | solution.py:20
  191.6 57.4 %reduce-scatter.14.cloned.1.call-start = ((), (), s32[]{:S(2)}) async-start(), calls=%async_computation.12 | async-start | bytes 368640 | tf_op jit(solution)/shard_map/reduce_scatter | solution.py:256
  199.5 75.5 %reduce-scatter.10.cloned.1.call-start = ((), (), s32[]{:S(2)}) async-start(), calls=%async_computation.10 | async-start | bytes 921600 | tf_op jit(solution)/shard_map/reduce_scatter | solution.py:250
  202.9 98.4 %reduce-scatter.16.cloned.1.call-start = ((), (), s32[]{:S(2)}) async-start(), calls=%async_computation.13 | async-start | bytes 921600 | tf_op jit(solution)/shard_map/reduce_scatter | solution.py:259
  204.2 130.3 %reduce-scatter.22.cloned.1.call-start = ((), (), s32[]{:S(2)}) async-start(), calls=%async_computation.16 | async-start | bytes 2457600
  208.5 158.2 %reduce-scatter.18.cloned.1.call-start = ((), (), s32[]{:S(2)}) async-start(), calls=%async_computation.14 | async-start | bytes 2211840 | tf_op jit(solution)/shard_map/reduce_scatter | solution.py:265
  211.5 187.1 %reduce-scatter.20.cloned.1.call-start = ((), (), s32[]{:S(2)}) async-start(), calls=%async_computation.15 | async-start | bytes 2211840 | tf_op jit(solution)/shard_map/reduce_scatter | solution.py:268
  (45 other events, 215.0 us)
Sparse Core Ops, SparseCore 0:
  9.6 25.8 all-gather.3
  37.0 20.3 all-gather.5
  63.5 30.5 all-gather.7
  191.8 34.4 reduce-scatter.11
  228.7 20.2 reduce-scatter.13
  252.0 22.9 reduce-scatter.9
  278.3 22.9 reduce-scatter.15
  303.9 30.6 reduce-scatter.21
  337.3 29.3 reduce-scatter.17
  369.2 29.3 reduce-scatter.19
where the time goes:
time: 556 us; the launch traced here: 555 us
  blocking collectives  203 us (37%)
  waiting for transfers between devices  191 us (34%)
  matrix products  69.2 us (12%)
  starting transfers between devices  34.4 us (6%)
  other arithmetic  24.3 us (4%)
  local copies, waits for them, and re-layouts  17 us (3%)
  between operations  16.5 us (3%)
    psum x1, blocking collectives, per_device(): lax.psum((owner_sums[0], owner_sums[1], owner_sums[2], owner_sums[3], own...  150 us
    unnamed x11, waiting for transfers between devices  34.8 us
    ppermute x16, starting transfers between devices, from_behind(): return lax.ppermute(block, axis, route)  34 us
    reduce_scatter x1, waiting for transfers between devices, per_device(): lax.psum_scatter(grad_up_w.astype(jnp.bfloat16), 'group', scatter_dimensi...  31.8 us
    reduce_scatter x1, waiting for transfers between devices, per_device(): lax.psum_scatter(grad_gate_w.astype(jnp.bfloat16), 'group', scatter_dimen...  30.9 us
    reduce_scatter x1, waiting for transfers between devices, per_device(): lax.psum_scatter(grad_out_w.astype(jnp.bfloat16), 'group', scatter_dimens...  26.3 us
    reduce_scatter x1, waiting for transfers between devices, per_device(): lax.psum_scatter(grad_query_w.astype(jnp.bfloat16), 'group', scatter_dime...  26 us
    ppermute x16, waiting for transfers between devices, from_behind(): return lax.ppermute(block, axis, route)  24.4 us
  transfers between devices with their start and end apart: 26, of which 12 were waited for; matrix products, arithmetic and copies ran while one was open for 9% of the time, Pallas kernels for 0%

commit v1 on v0

--- a/solution.py
+++ b/solution.py
@@ -1,8 +1,11 @@
+import functools
 import math
 
 import jax
 import jax.numpy as jnp
 from jax import lax
+from jax.experimental import pallas as pl
+from jax.experimental.pallas import tpu as pltpu
 from jax.sharding import PartitionSpec as P
 
 HEAD_DIM = 64
@@ -62,6 +65,472 @@
     )
     grad_gain = jnp.sum(grad_normed * value_matrix * scale_rows, axis=0)
     return (grad_values, grad_gain)
+
+
+MESH = pl.DeviceIdType.MESH
+VMEM_LIMIT = 56 * 1024 * 1024
+
+
+def flip_bit(index, bit):
+    return index + bit - 2 * bit * (lax.rem(lax.div(index, bit), 2))
+
+
+def greet(partners):
+    barrier = pltpu.get_barrier_semaphore()
+    for partner in partners:
+        pl.semaphore_signal(barrier, inc=1, device_id=partner, device_id_type=MESH)
+    pl.semaphore_wait(barrier, len(partners))
+
+
+def remote(source, target, send_sem, recv_sem, partner):
+    return pltpu.make_async_remote_copy(
+        src_ref=source,
+        dst_ref=target,
+        send_sem=send_sem,
+        recv_sem=recv_sem,
+        device_id=partner,
+        device_id_type=MESH,
+    )
+
+
+def gather_kernel(qkvo, gate, up, down, qkvo_all, gate_all, up_all, down_all, sends, recvs, local):
+    r = lax.axis_index("replica")
+    g = lax.axis_index("group")
+    core_partner = (r, flip_bit(g, 1))
+    y_partner = (r, flip_bit(g, 2))
+    x_partner = (flip_bit(r, 1), g)
+    x = lax.rem(r, 2)
+    across = flip_bit(g, 2)
+    greet((core_partner, y_partner, x_partner))
+    shards = (qkvo, gate, up, down)
+    wholes = (qkvo_all, gate_all, up_all, down_all)
+
+    def half(whole, owner, part):
+        if whole.shape[2] % 256 == 0:
+            width = whole.shape[2] // 2
+            return whole.at[owner, :, pl.ds(pl.multiple_of(part * width, 128), width)]
+        height = whole.shape[1] // 2
+        return whole.at[owner, pl.ds(pl.multiple_of(part * height, 16), height), :]
+
+    def half_shard(shard, part):
+        if shard.shape[1] % 256 == 0:
+            width = shard.shape[1] // 2
+            return shard.at[:, pl.ds(pl.multiple_of(part * width, 128), width)]
+        height = shard.shape[0] // 2
+        return shard.at[pl.ds(pl.multiple_of(part * height, 16), height), :]
+
+    started = []
+    locals_started = []
+    y_copies = []
+    for i in range(4):
+        copy = remote(
+            half_shard(shards[i], x), half(wholes[i], g, x), sends.at[i, 0], recvs.at[i, 0], y_partner
+        )
+        copy.start()
+        y_copies.append(copy)
+    core_copies = []
+    for i in range(4):
+        copy = remote(
+            shards[i], wholes[i].at[g], sends.at[i, 1], recvs.at[i, 1], core_partner
+        )
+        copy.start()
+        core_copies.append(copy)
+        own = pltpu.make_async_copy(shards[i], wholes[i].at[g], local.at[i])
+        own.start()
+        locals_started.append(own)
+    x_copies = []
+    for i in range(4):
+        y_copies[i].wait_recv()
+        piece = half(wholes[i], across, x)
+        copy = remote(piece, piece, sends.at[i, 2], recvs.at[i, 2], x_partner)
+        copy.start()
+        x_copies.append(copy)
+        copy = remote(piece, piece, sends.at[i, 3], recvs.at[i, 3], core_partner)
+        copy.start()
+        started.append(copy)
+    for i in range(4):
+        x_copies[i].wait_recv()
+        piece = half(wholes[i], across, 1 - x)
+        copy = remote(piece, piece, sends.at[i, 4], recvs.at[i, 4], core_partner)
+        copy.start()
+        started.append(copy)
+    for copy in locals_started:
+        copy.wait()
+    for copy in core_copies:
+        copy.wait()
+    for copy in started:
+        copy.wait()
+    for copy in y_copies + x_copies:
+        copy.wait_send()
+
+
+def gather_weights(qkvo, gate, up, down):
+    vmem = pl.BlockSpec(memory_space=pltpu.VMEM)
+    arrays = (qkvo, gate, up, down)
+    return pl.pallas_call(
+        gather_kernel,
+        out_shape=[jax.ShapeDtypeStruct((4,) + a.shape, a.dtype) for a in arrays],
+        in_specs=[vmem] * 4,
+        out_specs=[vmem] * 4,
+        scratch_shapes=[
+            pltpu.SemaphoreType.DMA((4, 5)),
+            pltpu.SemaphoreType.DMA((4, 5)),
+            pltpu.SemaphoreType.DMA((4,)),
+        ],
+        compiler_params=pltpu.CompilerParams(
+            collective_id=1, has_side_effects=True, vmem_limit_bytes=VMEM_LIMIT
+        ),
+    )(*arrays)
+
+
+def ring_partner(offset):
+    groups = lax.axis_size("group")
+    total = lax.axis_size("replica") * groups
+    here = lax.axis_index("replica") * groups + lax.axis_index("group")
+    there = lax.rem(here + offset + total, total)
+    return (lax.div(there, groups), lax.rem(there, groups))
+
+
+def window_kernel(reach, packed, window, sends, recvs, local):
+    barrier = pltpu.get_barrier_semaphore()
+    for offset in range(1, reach + 1):
+        pl.semaphore_signal(barrier, inc=1, device_id=ring_partner(-offset), device_id_type=MESH)
+    pl.semaphore_wait(barrier, reach)
+    copies = []
+    for offset in range(reach, 0, -1):
+        copy = remote(
+            packed,
+            window.at[reach - offset],
+            sends.at[offset - 1],
+            recvs.at[offset - 1],
+            ring_partner(offset),
+        )
+        copy.start()
+        copies.append(copy)
+    own = pltpu.make_async_copy(packed, window.at[reach], local)
+    own.start()
+    own.wait()
+    for copy in copies:
+        copy.wait()
+
+
+def exchange_window(packed, reach):
+    vmem = pl.BlockSpec(memory_space=pltpu.VMEM)
+    return pl.pallas_call(
+        functools.partial(window_kernel, reach),
+        out_shape=jax.ShapeDtypeStruct((reach + 1,) + packed.shape, packed.dtype),
+        in_specs=[vmem],
+        out_specs=vmem,
+        scratch_shapes=[
+            pltpu.SemaphoreType.DMA((reach,)),
+            pltpu.SemaphoreType.DMA((reach,)),
+            pltpu.SemaphoreType.DMA,
+        ],
+        compiler_params=pltpu.CompilerParams(
+            collective_id=2, has_side_effects=True, vmem_limit_bytes=VMEM_LIMIT
+        ),
+    )(packed)
+
+
+def return_kernel(reach, window, own, total, landed, sends, recvs):
+    barrier = pltpu.get_barrier_semaphore()
+    for offset in range(1, reach + 1):
+        pl.semaphore_signal(barrier, inc=1, device_id=ring_partner(offset), device_id_type=MESH)
+    pl.semaphore_wait(barrier, reach)
+    copies = []
+    for offset in range(reach, 0, -1):
+        copy = remote(
+            window.at[reach - offset],
+            landed.at[offset - 1],
+            sends.at[offset - 1],
+            recvs.at[offset - 1],
+            ring_partner(-offset),
+        )
+        copy.start()
+        copies.append(copy)
+    for copy in copies:
+        copy.wait()
+    tally = own[...]
+    for offset in range(reach):
+        tally = tally + landed[offset].astype(jnp.float32)
+    total[...] = tally
+
+
+def return_window(window, own):
+    reach = window.shape[0]
+    vmem = pl.BlockSpec(memory_space=pltpu.VMEM)
+    return pl.pallas_call(
+        functools.partial(return_kernel, reach),
+        out_shape=jax.ShapeDtypeStruct(own.shape, jnp.float32),
+        in_specs=[vmem, vmem],
+        out_specs=vmem,
+        scratch_shapes=[
+            pltpu.VMEM(window.shape, window.dtype),
+            pltpu.SemaphoreType.DMA((reach,)),
+            pltpu.SemaphoreType.DMA((reach,)),
+        ],
+        compiler_params=pltpu.CompilerParams(
+            collective_id=3, has_side_effects=True, vmem_limit_bytes=VMEM_LIMIT
+        ),
+    )(window, own)
+
+
+CHUNKS = 3
+TILES = 16
+
+
+def reduce_kernel(
+    replicas,
+    normed_two_t,
+    normed_one_t,
+    attended_t,
+    out_grad_t,
+    grad_gate,
+    grad_up,
+    grad_qkvo,
+    hidden,
+    gains,
+    out_wide,
+    out_down,
+    out_gains,
+    parts,
+    from_core,
+    from_y,
+    from_x,
+    from_z,
+    from_far,
+    final,
+    tally,
+    from_gain,
+    sends,
+    recvs,
+    gain_sends,
+    gain_recvs,
+):
+    r = lax.axis_index("replica")
+    g = lax.axis_index("group")
+    c = lax.rem(g, 2)
+    y = lax.div(g, 2)
+    x = lax.rem(r, 2)
+    z = lax.rem(lax.div(r, 2), 4)
+    base = r - 2 * z
+    core_partner = (r, flip_bit(g, 1))
+    y_partner = (r, flip_bit(g, 2))
+    x_partner = (flip_bit(r, 1), g)
+    z_partners = [(base + 2 * lax.rem(z + d, 4), g) for d in (1, 2, 3)]
+    far_bits = []
+    bit = 8
+    while bit < replicas:
+        far_bits.append(bit)
+        bit *= 2
+    far_partners = [(flip_bit(r, bit), g) for bit in far_bits]
+    greet([core_partner, y_partner, x_partner] + z_partners + far_partners)
+    half = TILES // 2
+    piece = TILES // 8
+    lefts = (normed_two_t, normed_two_t, normed_one_t)
+    rights = (grad_gate, grad_up, grad_qkvo)
+    pending = []
+
+    def start(chunk, slot, source, target, partner):
+        copy = remote(source, target, sends.at[chunk, slot], recvs.at[chunk, slot], partner)
+        copy.start()
+        pending.append(copy)
+        return copy
+
+    gain_slot = [0]
+
+    def gain_start(target, partner):
+        slot = gain_slot[0]
+        gain_slot[0] += 1
+        copy = remote(tally.at[target], from_gain.at[slot], gain_sends.at[slot], gain_recvs.at[slot], partner)
+        copy.start()
+        pending.append(copy)
+        return (copy, slot)
+
+    def stage_product(k):
+        for pair in range(6):
+            columns = slice(pair * 256, pair * 256 + 256)
+            right = rights[k][:, columns]
+            if k == 2 and pair >= 4:
+                product = jnp.dot(attended_t[...], right, preferred_element_type=jnp.float32)
+            else:
+                product = jnp.dot(lefts[k][...], right, preferred_element_type=jnp.float32)
+            if k == 2 and pair == 3:
+                other = jnp.dot(attended_t[...], right, preferred_element_type=jnp.float32)
+                lane = lax.broadcasted_iota(jnp.int32, product.shape, 1)
+                product = jnp.where(lane < 960 - 768, product, other)
+            product = product.astype(jnp.bfloat16)
+            for s in range(4):
+                rows = product[144 * s : 144 * s + 144]
+                parts[s % 2, s // 2, k, 2 * pair] = rows[:, :128]
+                parts[s % 2, s // 2, k, 2 * pair + 1] = rows[:, 128:]
+        for s in range(4):
+            columns = slice(s * 384 + k * 128, s * 384 + k * 128 + 128)
+            product = jnp.dot(
+                out_grad_t[...], hidden[:, columns], preferred_element_type=jnp.float32
+            ).astype(jnp.bfloat16)
+            for row in range(4):
+                parts[s % 2, s // 2, k, 12 + row] = product[144 * row : 144 * row + 144]
+        return start(k, 0, parts.at[1 - c, :, k], from_core.at[k], core_partner)
+
+    def stage_y(k, arrived):
+        arrived.wait_recv()
+
+        def add(t, carry):
+            for yy in range(2):
+                parts[c, yy, k, t] = (
+                    parts[c, yy, k, t].astype(jnp.float32) + from_core[k, yy, t].astype(jnp.float32)
+                ).astype(jnp.bfloat16)
+            return carry
+
+        lax.fori_loop(0, TILES, add, 0)
+        return start(k, 1, parts.at[c, 1 - y, k], from_y.at[k], y_partner)
+
+    def stage_x(k, arrived):
+        arrived.wait_recv()
+
+        def add(t, carry):
+            parts[c, y, k, t] = (
+                parts[c, y, k, t].astype(jnp.float32) + from_y[k, t].astype(jnp.float32)
+            ).astype(jnp.bfloat16)
+            return carry
+
+        lax.fori_loop(0, TILES, add, 0)
+        return start(
+            k, 2, parts.at[c, y, k, pl.ds((1 - x) * half, half)], from_x.at[k], x_partner
+        )
+
+    def stage_z(k, arrived):
+        arrived.wait_recv()
+
+        def add(t, carry):
+            parts[c, y, k, x * half + t] = (
+                parts[c, y, k, x * half + t].astype(jnp.float32) + from_x[k, t].astype(jnp.float32)
+            ).astype(jnp.bfloat16)
+            return carry
+
+        lax.fori_loop(0, half, add, 0)
+        copies = []
+        for d in range(1, 4):
+            there = lax.rem(z + d, 4)
+            copies.append(
+                start(
+                    k,
+                    2 + d,
+                    parts.at[c, y, k, pl.ds(x * half + there * piece, piece)],
+                    from_z.at[k, d - 1],
+                    z_partners[d - 1],
+                )
+            )
+        return copies
+
+    def stage_back(k, arrived):
+        for copy in arrived:
+            copy.wait_recv()
+        spot = x * half + z * piece
+        for t in range(piece):
+            total = parts[c, y, k, spot + t].astype(jnp.float32)
+            for d in range(3):
+                total = total + from_z[k, d, t].astype(jnp.float32)
+            final[k, spot + t] = total.astype(jnp.bfloat16)
+        for step in range(len(far_bits)):
+            from_far[k, 2 * step] = final[k, pl.ds(spot, piece)]
+            copy = start(
+                k,
+                9 + step,
+                from_far.at[k, 2 * step],
+                from_far.at[k, 2 * step + 1],
+                far_partners[step],
+            )
+            copy.wait_recv()
+            for t in range(piece):
+                final[k, spot + t] = (
+                    final[k, spot + t].astype(jnp.float32)
+                    + from_far[k, 2 * step + 1, t].astype(jnp.float32)
+                ).astype(jnp.bfloat16)
+        own = final.at[k, pl.ds(spot, piece)]
+        return [start(k, 5 + d, own, own, z_partners[d - 1]) for d in range(1, 4)]
+
+    def stage_back_x(k, arrived):
+        for copy in arrived:
+            copy.wait_recv()
+        own = final.at[k, pl.ds(x * half, half)]
+        return start(k, 9 + len(far_bits), own, own, x_partner)
+
+    def stage_out(k, arrived):
+        arrived.wait_recv()
+        for t in range(12):
+            out_wide[k, :, t * 128 : t * 128 + 128] = final[k, t].astype(jnp.float32)
+        column = jnp.concatenate(
+            [final[k, 12 + row].astype(jnp.float32) for row in range(4)], axis=0
+        )
+        out_down[k * 128 : k * 128 + 128, :] = column.T
+
+    stages = (stage_product, stage_y, stage_x, stage_z, stage_back, stage_back_x, stage_out)
+    state = [None] * CHUNKS
+
+    gain_steps = [[core_partner], [y_partner], [x_partner], z_partners] + [[p] for p in far_partners]
+    tally[0] = gains[...]
+    gain_flight = []
+    for t in range(CHUNKS + len(stages) - 1):
+        for k in range(CHUNKS):
+            s = t - k
+            if s == 0:
+                state[k] = stage_product(k)
+            elif 0 < s < len(stages):
+                state[k] = stages[s](k, state[k])
+        if t <= len(gain_steps):
+            if gain_flight:
+                total = tally[t - 1]
+                for copy, slot in gain_flight:
+                    copy.wait_recv()
+                    total = total + from_gain[slot]
+                if t < len(gain_steps):
+                    tally[t] = total
+                else:
+                    out_gains[...] = total
+                gain_flight = []
+            if t < len(gain_steps):
+                gain_flight = [gain_start(t, p) for p in gain_steps[t]]
+    for copy in pending:
+        copy.wait_send()
+
+
+def reduce_gradients(replicas, *operands):
+    vmem = pl.BlockSpec(memory_space=pltpu.VMEM)
+    far = max(replicas.bit_length() - 4, 0)
+    slots = 10 + far
+    gain_slots = 6 + far
+    tile = (144, 128)
+    low = jnp.bfloat16
+    return pl.pallas_call(
+        functools.partial(reduce_kernel, replicas),
+        out_shape=[
+            jax.ShapeDtypeStruct((CHUNKS, 144, 1536), jnp.float32),
+            jax.ShapeDtypeStruct((384, 576), jnp.float32),
+            jax.ShapeDtypeStruct((8, 256), jnp.float32),
+        ],
+        in_specs=[vmem] * 9,
+        out_specs=[vmem] * 3,
+        scratch_shapes=[
+            pltpu.VMEM((2, 2, CHUNKS, TILES) + tile, low),
+            pltpu.VMEM((CHUNKS, 2, TILES) + tile, low),
+            pltpu.VMEM((CHUNKS, TILES) + tile, low),
+            pltpu.VMEM((CHUNKS, TILES // 2) + tile, low),
+            pltpu.VMEM((CHUNKS, 3, TILES // 8) + tile, low),
+            pltpu.VMEM((CHUNKS, 2 * max(far, 1), TILES // 8) + tile, low),
+            pltpu.VMEM((CHUNKS, TILES) + tile, low),
+            pltpu.VMEM((4 + far, 8, 256), jnp.float32),
+            pltpu.VMEM((gain_slots, 8, 256), jnp.float32),
+            pltpu.SemaphoreType.DMA((CHUNKS, slots)),
+            pltpu.SemaphoreType.DMA((CHUNKS, slots)),
+            pltpu.SemaphoreType.DMA((gain_slots,)),
+            pltpu.SemaphoreType.DMA((gain_slots,)),
+        ],
+        compiler_params=pltpu.CompilerParams(
+            collective_id=4, has_side_effects=True, vmem_limit_bytes=VMEM_LIMIT
+        ),
+    )(*operands)
 
 
 def per_device(
@@ -79,27 +548,18 @@
     down_w,
     out_grad,
 ):
-    (
-        gain_one_all,
-        query_all,
-        key_all,
-        value_all,
-        out_all,
-        gain_two_all,
-        gate_all,
-        up_all,
-        down_all,
-    ) = (
-        lax.all_gather(gain_one, "group", axis=0, tiled=True),
-        lax.all_gather(query_w, "group", axis=0, tiled=True),
-        lax.all_gather(key_w, "group", axis=0, tiled=True),
-        lax.all_gather(value_weight, "group", axis=0, tiled=True),
-        lax.all_gather(out_w, "group", axis=0, tiled=True),
-        lax.all_gather(gain_two, "group", axis=0, tiled=True),
-        lax.all_gather(gate_w, "group", axis=0, tiled=True),
-        lax.all_gather(up_w, "group", axis=0, tiled=True),
-        lax.all_gather(down_w, "group", axis=0, tiled=True),
-    )
+    qkvo_all, gate_all, up_all, down_all = gather_weights(
+        jnp.concatenate([query_w, key_w, value_weight, out_w], axis=1), gate_w, up_w, down_w
+    )
+    qkvo_all, gate_all, up_all, down_all = (
+        a.reshape(a.shape[0] * a.shape[1], a.shape[2]) for a in (qkvo_all, gate_all, up_all, down_all)
+    )
+    joined_w = qkvo_all[:, : query_w.shape[1] + 2 * key_w.shape[1]]
+    out_all = qkvo_all[:, query_w.shape[1] + 2 * key_w.shape[1] :]
+    query_all = qkvo_all[:, : query_w.shape[1]]
+    key_all = qkvo_all[:, query_w.shape[1] : query_w.shape[1] + key_w.shape[1]]
+    gain_one_all = lax.all_gather(gain_one, "group", axis=0, tiled=True)
+    gain_two_all = lax.all_gather(gain_two, "group", axis=0, tiled=True)
     tok_rows = inputs.shape[0]
     query_heads = query_all.shape[1] // HEAD_DIM
     kv_heads = key_all.shape[1] // HEAD_DIM
@@ -123,7 +583,6 @@
     scale_one = rms_scale(inputs_wide)
     gain_one_wide = gain_one_all.astype(jnp.float32)
     first_normed = (inputs_wide * scale_one * gain_one_wide).astype(jnp.bfloat16)
-    joined_w = jnp.concatenate([query_all, key_all, value_all], axis=1)
     projected = jnp.dot(first_normed, joined_w, preferred_element_type=jnp.float32)
     query_cols = query_heads * HEAD_DIM
     queries = apply_rotary(
@@ -136,10 +595,7 @@
     key_matrix = key_matrix.astype(jnp.bfloat16).reshape(tok_rows, kv_width)
     value_matrix = projected[:, query_cols + kv_width :].astype(jnp.bfloat16)
     packed = jnp.concatenate([key_matrix, value_matrix], axis=1)
-    blocks = [packed]
-    for offset in range(1, reach_back + 1):
-        blocks.insert(0, from_behind(packed, ("replica", "group"), offset))
-    window = jnp.concatenate(blocks, axis=0)
+    window = exchange_window(packed, reach_back).reshape(window_rows, 2 * kv_width)
     key_grid = window[:, :kv_width].reshape(window_rows, kv_heads, HEAD_DIM)
     value_grid = window[:, kv_width:].reshape(window_rows, kv_heads, HEAD_DIM)
     query_grid = queries.reshape(tok_rows, kv_heads, repeat_heads, HEAD_DIM)
@@ -210,14 +666,12 @@
         ],
         axis=1,
     )
-    own_grad = grad_window[reach_back * tok_rows :]
-    for offset in range(1, reach_back + 1):
-        lower_edge = (reach_back - offset) * tok_rows
-        own_grad = own_grad + from_behind(
-            grad_window[lower_edge : lower_edge + tok_rows].astype(jnp.bfloat16),
-            ("replica", "group"),
-            -offset,
-        ).astype(jnp.float32)
+    own_grad = return_window(
+        grad_window[: reach_back * tok_rows]
+        .astype(jnp.bfloat16)
+        .reshape(reach_back, tok_rows, 2 * kv_width),
+        grad_window[reach_back * tok_rows :],
+    )
     grad_keys = apply_rotary(
         own_grad[:, :kv_width].reshape(tok_rows, kv_heads, HEAD_DIM), -rotary_angles
     )
@@ -227,77 +681,44 @@
         grad_query_rot.reshape(tok_rows, query_heads, HEAD_DIM), -rotary_angles
     )
     grad_queries = grad_queries.reshape(tok_rows, query_cols).astype(jnp.bfloat16)
-    grad_normed_one = (
-        times_transpose(grad_queries, query_all)
-        + times_transpose(grad_keys, key_all)
-        + times_transpose(grad_values, value_all)
-    )
+    grad_qkv = jnp.concatenate([grad_queries, grad_keys, grad_values], axis=1)
+    grad_normed_one = times_transpose(grad_qkv, joined_w)
     grad_inputs_norm, grad_gain_one = norm_back(
         grad_normed_one, inputs_wide, scale_one, gain_one_wide
     )
     grad_inputs = grad_middle + grad_inputs_norm
-    grad_query_w = contract_rows(first_normed, grad_queries)
-    grad_key_w = contract_rows(first_normed, grad_keys)
-    grad_value_w = contract_rows(first_normed, grad_values)
-    grad_out_w = contract_rows(attended, grad_branch)
-    grad_gate_w = contract_rows(normed_two, grad_gate)
-    grad_up_w = contract_rows(normed_two, grad_up)
-    grad_down_w = contract_rows(hidden, out_grad)
-    owner_sums = (
-        lax.psum_scatter(
-            grad_gain_one.astype(jnp.bfloat16), "group", scatter_dimension=0, tiled=True
-        ).astype(jnp.float32),
-        lax.psum_scatter(
-            grad_query_w.astype(jnp.bfloat16), "group", scatter_dimension=0, tiled=True
-        ).astype(jnp.float32),
-        lax.psum_scatter(
-            grad_key_w.astype(jnp.bfloat16), "group", scatter_dimension=0, tiled=True
-        ).astype(jnp.float32),
-        lax.psum_scatter(
-            grad_value_w.astype(jnp.bfloat16), "group", scatter_dimension=0, tiled=True
-        ).astype(jnp.float32),
-        lax.psum_scatter(
-            grad_out_w.astype(jnp.bfloat16), "group", scatter_dimension=0, tiled=True
-        ).astype(jnp.float32),
-        lax.psum_scatter(
-            grad_gain_two.astype(jnp.bfloat16), "group", scatter_dimension=0, tiled=True
-        ).astype(jnp.float32),
-        lax.psum_scatter(
-            grad_gate_w.astype(jnp.bfloat16), "group", scatter_dimension=0, tiled=True
-        ).astype(jnp.float32),
-        lax.psum_scatter(
-            grad_up_w.astype(jnp.bfloat16), "group", scatter_dimension=0, tiled=True
-        ).astype(jnp.float32),
-        lax.psum_scatter(
-            grad_down_w.astype(jnp.bfloat16), "group", scatter_dimension=0, tiled=True
-        ).astype(jnp.float32),
-    )
-    totals = lax.psum(
-        (
-            owner_sums[0],
-            owner_sums[1],
-            owner_sums[2],
-            owner_sums[3],
-            owner_sums[4],
-            owner_sums[5],
-            owner_sums[6],
-            owner_sums[7],
-            owner_sums[8],
-        ),
-        "replica",
-    )
+    width = gain_one_all.shape[0]
+    gain_grads = jnp.pad(jnp.concatenate([grad_gain_one, grad_gain_two]), (0, 2048 - 2 * width))
+    wide, grad_down_w, gain_sums = reduce_gradients(
+        lax.axis_size("replica"),
+        normed_two.T,
+        first_normed.T,
+        attended.T,
+        out_grad.T,
+        grad_gate,
+        grad_up,
+        jnp.concatenate([grad_qkv, grad_branch], axis=1),
+        hidden,
+        gain_grads.reshape(8, 256),
+    )
+    gain_sums = gain_sums.reshape(2048)[: 2 * width].reshape(2, width)
+    shard = width // lax.axis_size("group")
+    gain_sums = lax.dynamic_slice_in_dim(gain_sums, lax.axis_index("group") * shard, shard, 1)
+    first = query_cols
+    second = first + kv_width
+    third = second + kv_width
     return (
         outputs,
         grad_inputs,
-        totals[0],
-        totals[1],
-        totals[2],
-        totals[3],
-        totals[4],
-        totals[5],
-        totals[6],
-        totals[7],
-        totals[8],
+        gain_sums[0],
+        wide[2, :, :first],
+        wide[2, :, first:second],
+        wide[2, :, second:third],
+        wide[2, :, third:],
+        gain_sums[1],
+        wide[0],
+        wide[1],
+        grad_down_w,
     )
 
 

time: 556 us -> 341 us (0.61)
  Pallas kernels: 0 us -> 201 us
  blocking collectives: 203 us -> 6.2 us
  waiting for transfers between devices: 191 us -> 0 us
  starting transfers between devices: 34.4 us -> 0 us
  local copies, waits for them, and re-layouts: 17 us -> 42.2 us
  between operations: 16.5 us -> 2.06 us
  matrix products: 69.2 us -> 60.2 us
    pallas_call x0 -> x4, Pallas kernels: none -> 201 us  [the longest x1 84.8 us: reduce_gradients(): pl.pallas_call(functools.partial(reduce_kernel, replicas), out_shape=[jax...]
    psum x1 -> x0, blocking collectives: 150 us -> none  [per_device(): lax.psum((owner_sums[0], owner_sums[1], owner_sums[2], owner_sums[3], own...]
    reduce_scatter x6 -> x0, waiting for transfers between devices: 132 us -> none  [the longest x1 31.8 us: per_device(): lax.psum_scatter(grad_up_w.astype(jnp.bfloat16), 'group', scatter_dimensi...]
    unnamed x11 -> x0, waiting for transfers between devices: 34.8 us -> none
    ppermute x16 -> x0, starting transfers between devices: 34 us -> none  [from_behind(): return lax.ppermute(block, axis, route)]
    all_gather x4 -> x0, blocking collectives: 32.2 us -> none  [the longest x1 9.06 us: per_device(): lax.all_gather(out_w, 'group', axis=0, tiled=True)]
    ppermute x16 -> x0, waiting for transfers between devices: 24.4 us -> none  [from_behind(): return lax.ppermute(block, axis, route)]
    unnamed x2 -> x1, blocking collectives: 20.8 us -> 6.2 us
  transfers between devices with their start and end apart: 26 -> 0, of which waited for: 12 -> 0; matrix products, arithmetic and copies ran while one was open for 9% -> 0% of each run, Pallas kernels for 0% -> 0%
where the time goes in v1:
time: 341 us; the launch traced here: 339 us
  Pallas kernels  201 us (59%)
  matrix products  60.2 us (18%)
  local copies, waits for them, and re-layouts  42.2 us (12%)
  other arithmetic  27.4 us (8%)
  blocking collectives  6.2 us (2%)
    pallas_call x1, Pallas kernels, reduce_gradients(): pl.pallas_call(functools.partial(reduce_kernel, replicas), out_shape=[jax...  84.8 us
    pallas_call x1, Pallas kernels, exchange_window(): pl.pallas_call(functools.partial(window_kernel, reach), out_shape=jax.Sha...  43.9 us
    pallas_call x1, Pallas kernels, gather_weights(): pl.pallas_call(gather_kernel, out_shape=[jax.ShapeDtypeStruct((4,) + a.sh...  36.8 us
    pallas_call x1, Pallas kernels, return_window(): pl.pallas_call(functools.partial(return_kernel, reach), out_shape=jax.Sha...  35.1 us
    unnamed x91, local copies, waits for them, and re-layouts  16.4 us
    convert_element_type x1, other arithmetic, per_device(): grad_scores = (probs * (grad_probs - inner)).astype(jnp.bfloat16)  14.2 us
    dot_general x1, matrix products, per_device(): jnp.einsum('tcrd,wcd->crtw', grad_attended, value_grid, preferred_element...  13.3 us
    dot_general x1, matrix products, per_device(): jnp.einsum('crtw,tcrd->wcd', probs_again, grad_attended, preferred_elemen...  11.6 us

profile of v1, /device:TPU:0, one launch (start us, length us, event | category | flops | bytes accessed | tf_op | source)
XLA Modules:
  0.0 338.9 jit_solution(4958803091965740012)
XLA Ops:
  0.7 2.1 concatenate.40.qkvo
  2.8 2.0 copy.113.down
  4.8 36.8 %shard_map.212 = (bf16[4,144,1536]{2,1,0:T(8,128)(2,1)}, bf16[4,144,1536]{2,1,0:T(8,128)(2,1)}, bf16[4,144,1536]{2,1,0:T(8,128)(2,1)}, bf16[4,384,576]{2,1,0:T(8,128)(2,1)}) custom-call(bf16[144,1536]{1,0:T(8,128)(2,1)} %concatenate.40.qkvo, bf16[144,1536]{1,0:T(8,128)(2,1)} %gate.1, bf16[144,1536]{1,0:T(8,128)(2,1)} %up.1, bf16[384,576]{1,0:T(8,128)(2,1)} %copy.113.down), custom_call_target="tpu_custom_call" | custom-call | tf_op jit(solution)/shard_map/pallas_call | solution.py:170
  43.6 6.2 %all-reduce.3 = (bf16[576]{0:T(1024)(128)(2,1)S(1)}, bf16[576]{0:T(1024)(128)(2,1)S(1)}) all-reduce(bf16[576]{0:T(1024)(128)(2,1)S(1)} %dynamic-update-slice, bf16[576]{0:T(1024)(128)(2,1)S(1)} %dynamic-update-slice.1), channel_id=1, replica_groups=mesh['replica'=8,'group'=4] {'group'}, use_global_device_ids=true, to_apply=%add.1 | all-reduce | flops 1152 | bytes 4608
  50.6 2.0 fusion.15
  54.2 43.9 %shard_map.213 = bf16[9,256,384]{2,1,0:T(8,128)(2,1)} custom-call(bf16[256,384]{1,0:T(8,128)(2,1)} %pad_maximum_fusion.3.packed), custom_call_target="tpu_custom_call" | custom-call | tf_op jit(solution)/shard_map/pallas_call | solution.py:219
  98.1 2.1 fusion.41
  104.2 3.3 fusion.43
  107.5 2.9 fusion.3
  110.5 4.1 %copy-done = f32[3,3,256,2304]{2,3,1,0:T(8,128)} copy-done((f32[3,3,256,2304]{2,3,1,0:T(8,128)}, f32[3,3,256,2304]{2,3,1,0:T(8,128)S(1)}, u32[]{:S(2)}) %copy-start) | copy-done | bytes 21233688
  114.6 4.1 %fusion.12 = bf16[3,64,3,256]{3,1,2,0:T(8,128)(2,1)S(1)} fusion(bf16[2304,3,64,1]{0,2,3,1:T(8,128)(2,1)S(1)} %bitcast.113, f32[3,3,256,2304]{2,3,1,0:T(8,128)S(1)} %get-tuple-element.109, f32[3,3,256]{2,1,0:T(4,128)S(1)} %fusion.3, f32[3,3,256]{2,1,0:T(4,128)S(1)} %get-tuple-element.108), kind=kOutput, calls=%fused_computation.36 | convolution fusion | flops 695549952 | bytes 22431744 | tf_op jit(solution)/shard_map/crtw,wcd->tcrd/dot_general | solution.py:616
  118.7 2.0 multiply_reduce_fusion.2
  123.8 2.6 multiply_convert_fusion
  127.3 1.7 convolution_add_fusion
  128.9 2.1 copy.138
  131.0 2.6 fusion.46
  133.6 2.3 multiply_reduce_fusion
  137.2 2.1 fusion.40
  139.3 1.7 convolution_convert_fusion
  141.0 13.3 %fusion = (f32[3,3,256]{2,1,0:T(4,128)S(1)}, f32[3,2304,256,3]{2,1,3,0:T(8,128)}) fusion(f32[3,3,256,2304]{2,3,1,0:T(8,128)} %copy-done, f32[3,3,256]{2,1,0:T(4,128)S(1)} %log_add_fusion, bf16[2304,3,64,1]{0,2,3,1:T(8,128)(2,1)S(1)} %bitcast.114, bf16[256,3,3,64]{0,3,2,1:T(8,128)(2,1)S(1)} %bitcast.124), kind=kOutput, calls=%fused_computation.2 | convolution fusion | flops 695400192 | bytes 43665408 | tf_op jit(solution)/shard_map/tcrd,wcd->crtw/dot_general | solution.py:646
  154.4 14.2 %fusion.2 = bf16[3,3,256,2304]{2,3,1,0:T(8,128)(2,1)S(1)} fusion(f32[3,2304,256,3]{2,1,3,0:T(8,128)} %get-tuple-element.114, f32[3,3,256,2304]{2,3,1,0:T(8,128)} %copy-done, f32[3,3,256]{2,1,0:T(4,128)S(1)} %get-tuple-element.113, f32[3,3,256]{2,1,0:T(4,128)S(1)} %log_add_fusion), kind=kLoop, calls=%fused_computation.4 | loop fusion | flops 21233664 | bytes 53102592 | tf_op jit(solution)/shard_map/convert_element_type | solution.py:650
  168.6 4.5 %fusion.9 = f32[3,64,2304]{2,1,0:T(8,128)} fusion(bf16[3,3,256,2304]{2,3,1,0:T(8,128)(2,1)S(1)} %fusion.2, bf16[256,3,3,32]{0,3,2,1:T(8,128)(2,1)S(1)} %bitcast.131, bf16[256,3,3,32]{0,3,2,1:T(8,128)(2,1)S(1)} %bitcast.129), kind=kOutput, calls=%fused_computation.15 | convolution fusion | flops 680509440 | bytes 12681216 | tf_op jit(solution)/shard_map/crtw,tcrd->wcd/dot_general | solution.py:656
  173.2 2.2 copy.128
  175.4 11.6 %fusion.5 = f32[3,64,2304,1]{2,1,3,0:T(8,128)} fusion(bf16[256,3,3,64]{0,3,2,1:T(8,128)(2,1)S(1)} %bitcast.125, f32[3,3,256,2304]{2,3,1,0:T(8,128)} %copy-done, f32[3,3,256]{2,1,0:T(4,128)S(1)} %log_add_fusion), kind=kOutput, calls=%fused_computation.11 | convolution fusion | flops 690094080 | bytes 23307264 | tf_op jit(solution)/shard_map/crtw,tcrd->wcd/dot_general | solution.py:659
  187.0 3.0 copy.129
  190.0 3.4 fusion.11
  194.3 35.1 %shard_map.214 = f32[256,384]{1,0:T(8,128)} custom-call(bf16[8,256,384]{2,1,0:T(8,128)(2,1)} %bitcast.110, f32[256,384]{1,0:T(8,128)} %pad_maximum_fusion.own), custom_call_target="tpu_custom_call" | custom-call | tf_op jit(solution)/shard_map/pallas_call | solution.py:262
  231.8 6.1 %convolution_multiply_fusion = f32[3,64,3,256]{3,1,2,0:T(8,128)S(1)} fusion(bf16[2304,3,64,1]{0,2,3,1:T(8,128)(2,1)S(1)} %bitcast.112, bf16[3,3,256,2304]{2,3,1,0:T(8,128)(2,1)} %copy-done.1), kind=kOutput, calls=%fused_computation.34 | convolution fusion | flops 679624704 | bytes 12091392 | tf_op jit(solution)/shard_map/crtw,wcd->tcrd/dot_general | solution.py:652
  244.7 84.8 %shard_map.215 = (f32[3,144,1536]{2,1,0:T(8,128)}, f32[384,576]{1,0:T(8,128)}, f32[8,256]{1,0:T(8,128)}) custom-call(bf16[576,256]{1,0:T(8,128)(2,1)} %copy.136.normed_two_t, bf16[576,256]{1,0:T(8,128)(2,1)} %copy.137.normed_one_t, bf16[576,256]{1,0:T(8,128)(2,1)} %bitcast.136, bf16[576,256]{1,0:T(8,128)(2,1)} %bitcast.121, ...), custom_call_target="tpu_custom_call" | custom-call | tf_op jit(solution)/shard_map/pallas_call | solution.py:506
  330.9 2.1 slice_bitcast_fusion.2
  333.0 1.9 slice_bitcast_fusion.4
  334.9 2.7 slice_bitcast_fusion
  (135 shorter events, 25.0 us)
Async XLA Ops:
  0.6 41.2 %copy-start.38 = (u32[32]{0:T(128)S(1)}, u32[32]{0:T(128)}, u32[]{:S(2)}) copy-start(u32[32]{0:T(128)} %constant.51) | copy-start | bytes 388
  0.7 41.0 %copy-start.24 = (bf16[256,576]{0,1:T(8,128)(2,1)S(1)}, bf16[256,576]{0,1:T(8,128)(2,1)}, u32[]{:S(2)}) copy-start(bf16[256,576]{0,1:T(8,128)(2,1)} %param.13) | copy-start | bytes 884740
  0.7 42.5 %copy-start.36 = (bf16[144]{0:T(256)(128)(2,1)S(1)}, bf16[144]{0:T(256)(128)(2,1)}, u32[]{:S(2)}) copy-start(bf16[144]{0:T(256)(128)(2,1)} %param.16) | copy-start | bytes 868
  0.7 42.7 %copy-start.37 = (bf16[144]{0:T(256)(128)(2,1)S(1)}, bf16[144]{0:T(256)(128)(2,1)}, u32[]{:S(2)}) copy-start(bf16[144]{0:T(256)(128)(2,1)} %param.21) | copy-start | bytes 868
  41.8 11.4 %copy-start.8 = (bf16[256,576]{1,0:T(8,128)(2,1)}, bf16[256,576]{1,0:T(8,128)(2,1)S(1)}, u32[]{:S(2)}) copy-start(bf16[256,576]{1,0:T(8,128)(2,1)S(1)} %copy.112) | copy-start | bytes 884740
  41.9 10.9 %copy-start.33 = (s32[256]{0:T(256)S(1)}, s32[256]{0:T(256)}, u32[]{:S(2)}) copy-start(s32[256]{0:T(256)} %param.14) | copy-start | bytes 3076
  41.9 10.9 %copy-start.34 = (s32[6]{0:T(128)S(1)}, s32[6]{0:T(128)}, u32[]{:S(2)}) copy-start(s32[6]{0:T(128)} %param.15) | copy-start | bytes 76
  49.8 2.7 copy-start.27
  52.6 45.5 %copy-start.20 = (f32[256,960]{0,1:T(8,128)}, f32[256,960]{0,1:T(8,128)S(1)}, u32[]{:S(2)}) copy-start(f32[256,960]{0,1:T(8,128)S(1)} %fusion.15) | copy-start | bytes 2949124
  101.6 5.9 %copy-start.4 = (bf16[2304,192]{0,1:T(8,128)(2,1)}, bf16[2304,192]{0,1:T(8,128)(2,1)S(1)}, u32[]{:S(2)}) copy-start(bf16[2304,192]{0,1:T(8,128)(2,1)S(1)} %copy.117) | copy-start | bytes 2654212
  103.1 4.4 %copy-start.21 = (bf16[256,9,32]{0,2,1:T(8,128)(2,1)}, bf16[256,9,32]{0,2,1:T(8,128)(2,1)S(1)}, u32[]{:S(2)}) copy-start(bf16[256,9,32]{0,2,1:T(8,128)(2,1)S(1)} %get-tuple-element.91) | copy-start | bytes 442372
  107.5 7.1 %copy-start = (f32[3,3,256,2304]{2,3,1,0:T(8,128)}, f32[3,3,256,2304]{2,3,1,0:T(8,128)S(1)}, u32[]{:S(2)}) copy-start(f32[3,3,256,2304]{2,3,1,0:T(8,128)S(1)} %get-tuple-element.109) | copy-start | bytes 63700996
  114.6 4.1 %copy-start.25 = (f32[3,3,256]{2,1,0:T(4,128)}, f32[3,3,256]{2,1,0:T(4,128)S(1)}, u32[]{:S(2)}) copy-start(f32[3,3,256]{2,1,0:T(4,128)S(1)} %fusion.3) | copy-start | bytes 27652
  114.6 4.1 %copy-start.9 = (bf16[256,576]{1,0:T(8,128)(2,1)S(1)}, bf16[256,576]{1,0:T(8,128)(2,1)}, u32[]{:S(2)}) copy-start(bf16[256,576]{1,0:T(8,128)(2,1)} %copy-done.8) | copy-start | bytes 884740
  118.7 2.0 copy-start.23
  118.7 2.0 copy-start.13
  131.0 2.6 copy-start.6
  136.0 3.3 copy-start.26
  139.3 15.1 %copy-start.14 = (bf16[256,576]{1,0:T(8,128)(2,1)}, bf16[256,576]{1,0:T(8,128)(2,1)S(1)}, u32[]{:S(2)}) copy-start(bf16[256,576]{1,0:T(8,128)(2,1)S(1)} %get-tuple-element.75) | copy-start | bytes 884740
  141.0 13.4 %copy-start.17 = (bf16[256,576]{0,1:T(8,128)(2,1)}, bf16[256,576]{0,1:T(8,128)(2,1)S(1)}, u32[]{:S(2)}) copy-start(bf16[256,576]{0,1:T(8,128)(2,1)S(1)} %convolution_convert_fusion) | copy-start | bytes 884740
  154.4 14.3 %copy-start.22 = (bf16[256,9,32]{0,2,1:T(8,128)(2,1)S(1)}, bf16[256,9,32]{0,2,1:T(8,128)(2,1)}, u32[]{:S(2)}) copy-start(bf16[256,9,32]{0,2,1:T(8,128)(2,1)} %copy-done.21) | copy-start | bytes 442372
  168.6 4.6 %copy-start.1 = (bf16[3,3,256,2304]{2,3,1,0:T(8,128)(2,1)}, bf16[3,3,256,2304]{2,3,1,0:T(8,128)(2,1)S(1)}, u32[]{:S(2)}) copy-start(bf16[3,3,256,2304]{2,3,1,0:T(8,128)(2,1)S(1)} %fusion.2) | copy-start | bytes 31850500
  173.2 2.2 copy-start.18
  190.0 3.4 %copy-start.2 = (f32[2304,192]{1,0:T(8,128)S(1)}, f32[2304,192]{1,0:T(8,128)}, u32[]{:S(2)}) copy-start(f32[2304,192]{1,0:T(8,128)} %copy.129) | copy-start | bytes 5308420
  194.3 37.5 %copy-start.5 = (bf16[2304,192]{0,1:T(8,128)(2,1)S(1)}, bf16[2304,192]{0,1:T(8,128)(2,1)}, u32[]{:S(2)}) copy-start(bf16[2304,192]{0,1:T(8,128)(2,1)} %copy-done.4) | copy-start | bytes 2654212
  231.8 6.3 %copy-start.10 = (bf16[256,576]{1,0:T(8,128)(2,1)S(1)}, bf16[256,576]{1,0:T(8,128)(2,1)}, u32[]{:S(2)}) copy-start(bf16[256,576]{1,0:T(8,128)(2,1)} %copy-done.8) | copy-start | bytes 884740
  231.8 6.3 %copy-start.28 = (f32[576]{0:T(1024)S(1)}, f32[576]{0:T(1024)}, u32[]{:S(2)}) copy-start(f32[576]{0:T(1024)} %copy-done.27) | copy-start | bytes 6916
  231.8 6.3 %copy-start.32 = (f32[256]{0:T(256)S(1)}, f32[256]{0:T(256)}, u32[]{:S(2)}) copy-start(f32[256]{0:T(256)} %copy-done.31) | copy-start | bytes 3076
  231.8 6.3 %copy-start.35 = (bf16[4,144,1536]{2,1,0:T(8,128)(2,1)S(1)}, bf16[4,144,1536]{2,1,0:T(8,128)(2,1)}, u32[]{:S(2)}) copy-start(bf16[4,144,1536]{2,1,0:T(8,128)(2,1)} %get-tuple-element.18) | copy-start | bytes 5308420
  239.5 3.3 copy-start.15
  240.7 3.3 copy-start.29
  333.0 4.6 %copy-start.19 = (f32[384,576]{1,0:T(8,128)S(1)}, f32[384,576]{1,0:T(8,128)}, u32[]{:S(2)}) copy-start(f32[384,576]{1,0:T(8,128)} %get-tuple-element.68) | copy-start | bytes 2654212
  (7 other events, 9.7 us)

commit v2 on v0

v2 whole, which is shorter than its diff:
```python
import functools
import math

import jax
import jax.numpy as jnp
from jax import lax
from jax.experimental import pallas as pl
from jax.experimental.pallas import tpu as pltpu
from jax.sharding import PartitionSpec as P

HEAD_DIM = 64
SEQUENCE_LENGTH = 2048


epsilon = 1e-05
rope_base = 100000.0
masked_score = -1e30


def from_behind(block, axis, distance):
    devices = range(lax.axis_size(axis))
    route = [(i - distance, i) for i in devices if i - distance in devices]
    return lax.ppermute(block, axis, route)


def rms_scale(value_matrix):
    return lax.rsqrt(jnp.mean(value_matrix * value_matrix, axis=-1, keepdims=True) + epsilon)


def rope_angles(positions, head_size):
    frequency = jnp.exp(
        jnp.arange(0, head_size, 2, dtype=jnp.float32) * (-math.log(rope_base) / head_size)
    )
    return positions.astype(jnp.float32)[:, None] * frequency[None, :]


def apply_rotary(value_matrix, rotary_angles):
    middle_cut = value_matrix.shape[-1] // 2
    former = value_matrix[..., :middle_cut]
    latter = value_matrix[..., middle_cut:]
    cosine = jnp.cos(rotary_angles)[:, None, :]
    sine_part = jnp.sin(rotary_angles)[:, None, :]
    return jnp.concatenate(
        [former * cosine - latter * sine_part, latter * cosine + former * sine_part], axis=-1
    )


def contract_rows(former, latter):
    return lax.dot_general(
        former, latter, (((0,), (0,)), ((), ())), preferred_element_type=jnp.float32
    )


def times_transpose(former, latter):
    return lax.dot_general(
        former, latter, (((1,), (1,)), ((), ())), preferred_element_type=jnp.float32
    )


def norm_back(grad_normed, value_matrix, scale_rows, gain_wide):
    weighted = grad_normed * gain_wide
    cubed = scale_rows * scale_rows * scale_rows
    grad_values = scale_rows * weighted - value_matrix * cubed * jnp.mean(
        weighted * value_matrix, axis=-1, keepdims=True
    )
    grad_gain = jnp.sum(grad_normed * value_matrix * scale_rows, axis=0)
    return (grad_values, grad_gain)


MESH = pl.DeviceIdType.MESH
VMEM_LIMIT = 56 * 1024 * 1024


def flip_bit(index, bit):
    return index + bit - 2 * bit * (lax.rem(lax.div(index, bit), 2))


def greet(partners):
    barrier = pltpu.get_barrier_semaphore()
    for partner in partners:
        pl.semaphore_signal(barrier, inc=1, device_id=partner, device_id_type=MESH)
    pl.semaphore_wait(barrier, len(partners))


def remote(source, target, send_sem, recv_sem, partner):
    return pltpu.make_async_remote_copy(
        src_ref=source,
        dst_ref=target,
        send_sem=send_sem,
        recv_sem=recv_sem,
        device_id=partner,
        device_id_type=MESH,
    )


def gather_kernel(qkvo, gate, up, down, qkvo_all, gate_all, up_all, down_all, sends, recvs, local):
    r = lax.axis_index("replica")
    g = lax.axis_index("group")
    core_partner = (r, flip_bit(g, 1))
    y_partner = (r, flip_bit(g, 2))
    x_partner = (flip_bit(r, 1), g)
    x = lax.rem(r, 2)
    across = flip_bit(g, 2)
    greet((core_partner, y_partner, x_partner))
    shards = (qkvo, gate, up, down)
    wholes = (qkvo_all, gate_all, up_all, down_all)

    def half(whole, owner, part):
        if whole.shape[2] % 256 == 0:
            width = whole.shape[2] // 2
            return whole.at[owner, :, pl.ds(pl.multiple_of(part * width, 128), width)]
        height = whole.shape[1] // 2
        return whole.at[owner, pl.ds(pl.multiple_of(part * height, 16), height), :]

    def half_shard(shard, part):
        if shard.shape[1] % 256 == 0:
            width = shard.shape[1] // 2
            return shard.at[:, pl.ds(pl.multiple_of(part * width, 128), width)]
        height = shard.shape[0] // 2
        return shard.at[pl.ds(pl.multiple_of(part * height, 16), height), :]

    started = []
    locals_started = []
    y_copies = []
    for i in range(4):
        copy = remote(
            half_shard(shards[i], x), half(wholes[i], g, x), sends.at[i, 0], recvs.at[i, 0], y_partner
        )
        copy.start()
        y_copies.append(copy)
    core_copies = []
    for i in range(4):
        copy = remote(
            shards[i], wholes[i].at[g], sends.at[i, 1], recvs.at[i, 1], core_partner
        )
        copy.start()
        core_copies.append(copy)
        own = pltpu.make_async_copy(shards[i], wholes[i].at[g], local.at[i])
        own.start()
        locals_started.append(own)
    x_copies = []
    for i in range(4):
        y_copies[i].wait_recv()
        piece = half(wholes[i], across, x)
        copy = remote(piece, piece, sends.at[i, 2], recvs.at[i, 2], x_partner)
        copy.start()
        x_copies.append(copy)
        copy = remote(piece, piece, sends.at[i, 3], recvs.at[i, 3], core_partner)
        copy.start()
        started.append(copy)
    for i in range(4):
        x_copies[i].wait_recv()
        piece = half(wholes[i], across, 1 - x)
        copy = remote(piece, piece, sends.at[i, 4], recvs.at[i, 4], core_partner)
        copy.start()
        started.append(copy)
    for copy in locals_started:
        copy.wait()
    for copy in core_copies:
        copy.wait()
    for copy in started:
        copy.wait()
    for copy in y_copies + x_copies:
        copy.wait_send()


def gather_weights(qkvo, gate, up, down):
    vmem = pl.BlockSpec(memory_space=pltpu.VMEM)
    arrays = (qkvo, gate, up, down)
    return pl.pallas_call(
        gather_kernel,
        out_shape=[jax.ShapeDtypeStruct((4,) + a.shape, a.dtype) for a in arrays],
        in_specs=[vmem] * 4,
        out_specs=[vmem] * 4,
        scratch_shapes=[
            pltpu.SemaphoreType.DMA((4, 5)),
            pltpu.SemaphoreType.DMA((4, 5)),
            pltpu.SemaphoreType.DMA((4,)),
        ],
        compiler_params=pltpu.CompilerParams(
            collective_id=1, has_side_effects=True, vmem_limit_bytes=VMEM_LIMIT
        ),
    )(*arrays)


def place():
    r = lax.axis_index("replica")
    g = lax.axis_index("group")
    slabs = lax.axis_size("replica") // 2
    slab = lax.div(r, 2)
    return r, g, slabs, slab


def slot_of(block, here):
    return lax.rem(block - here + 8, 8)


def window_kernel(packed, window, sends, recvs, local):
    r, g, slabs, slab = place()
    x = lax.rem(r, 2)
    y = lax.div(g, 2)
    c = lax.rem(g, 2)
    rx, gy, gc = flip_bit(r, 1), flip_bit(g, 2), flip_bit(g, 1)
    here = x * 4 + g
    at_x, at_y, at_c = (1 - x) * 4 + g, x * 4 + gy, x * 4 + gc
    at_xy = (1 - x) * 4 + gy
    ahead = (2 * lax.rem(slab + 1, slabs) + x, g)
    behind = (2 * lax.rem(slab + slabs - 1, slabs) + x, g)
    barrier = pltpu.get_barrier_semaphore()
    for partner in ((rx, g), (r, gy), (r, gc), behind):
        pl.semaphore_signal(barrier, inc=1, device_id=partner, device_id_type=MESH)
    pl.semaphore_wait(barrier, 4)
    to_ahead = remote(packed, window.at[0], sends.at[0], recvs.at[0], ahead)
    to_ahead.start()
    firsts = []
    for i, (bit, partner, there) in enumerate(
        ((x, (rx, g), at_x), (y, (r, gy), at_y), (c, (r, gc), at_c))
    ):
        target = window.at[slot_of(here, there)]
        early = remote(packed, target, sends.at[1 + i], recvs.at[1 + i], partner)
        late = remote(window.at[0], target, sends.at[1 + i], recvs.at[1 + i], partner)
        firsts.append((bit, early, late))
    for bit, early, late in firsts:
        pl.when(bit == 0)(early.start)
    own = pltpu.make_async_copy(packed, window.at[8], local)
    own.start()
    to_ahead.wait_recv()
    for bit, early, late in firsts:
        pl.when(bit == 1)(late.start)
    firsts[0][1].wait_recv()
    slot_x = window.at[slot_of(at_x, here)]
    diagonal = remote(
        slot_x, window.at[slot_of(at_x, at_y)], sends.at[4], recvs.at[4], (r, gy)
    )
    diagonal.start()
    core_x = remote(slot_x, window.at[slot_of(at_x, at_c)], sends.at[5], recvs.at[5], (r, gc))
    core_x.start()
    firsts[1][1].wait_recv()
    slot_y = window.at[slot_of(at_y, here)]
    core_y = remote(slot_y, window.at[slot_of(at_y, at_c)], sends.at[6], recvs.at[6], (r, gc))
    core_y.start()
    diagonal.wait_recv()
    slot_xy = window.at[slot_of(at_xy, here)]
    core_xy = remote(slot_xy, window.at[slot_of(at_xy, at_c)], sends.at[7], recvs.at[7], (r, gc))
    core_xy.start()
    firsts[2][1].wait_recv()
    for copy in (core_x, core_y, core_xy):
        copy.wait_recv()
    own.wait()
    for copy in (to_ahead, firsts[0][1], firsts[1][1], firsts[2][1], diagonal, core_x, core_y, core_xy):
        copy.wait_send()


def exchange_window(packed):
    vmem = pl.BlockSpec(memory_space=pltpu.VMEM)
    return pl.pallas_call(
        window_kernel,
        out_shape=jax.ShapeDtypeStruct((9,) + packed.shape, packed.dtype),
        in_specs=[vmem],
        out_specs=vmem,
        scratch_shapes=[
            pltpu.SemaphoreType.DMA((8,)),
            pltpu.SemaphoreType.DMA((8,)),
            pltpu.SemaphoreType.DMA,
        ],
        compiler_params=pltpu.CompilerParams(
            collective_id=2, has_side_effects=True, vmem_limit_bytes=VMEM_LIMIT
        ),
    )(packed)


def return_kernel(window, total, outgoing, landed, sums, sends, recvs):
    r, g, slabs, slab = place()
    x = lax.rem(r, 2)
    y = lax.div(g, 2)
    c = lax.rem(g, 2)
    rx, gy, gc = flip_bit(r, 1), flip_bit(g, 2), flip_bit(g, 1)
    here = x * 4 + g
    at_x, at_y, at_c = (1 - x) * 4 + g, x * 4 + gy, x * 4 + gc
    at_xy = (1 - x) * 4 + gy
    far = [x * 4 + gc, x * 4 + flip_bit(gc, 2), (1 - x) * 4 + gc, (1 - x) * 4 + flip_bit(gc, 2)]
    ahead = (2 * lax.rem(slab + 1, slabs) + x, g)
    behind = (2 * lax.rem(slab + slabs - 1, slabs) + x, g)
    barrier = pltpu.get_barrier_semaphore()
    for partner in ((rx, g), (r, gy), (r, gc), ahead):
        pl.semaphore_signal(barrier, inc=1, device_id=partner, device_id_type=MESH)
    pl.semaphore_wait(barrier, 4)
    wide = jnp.float32
    low = jnp.bfloat16
    core = []
    for i in (3, 1, 2, 0):
        copy = remote(
            window.at[slot_of(far[i], here)], landed.at[i], sends.at[i], recvs.at[i], (r, gc)
        )
        copy.start()
        core.append(copy)

    def blend(bit, index):
        block = landed[index].astype(wide)
        zero = jnp.zeros_like(block)
        total[...] += jnp.where(bit == 0, block, zero)
        sums[...] += jnp.where(bit == 1, block, zero)

    core[0].wait_recv()
    outgoing[0] = (window[slot_of(at_xy, here)].astype(wide) + landed[3].astype(wide)).astype(low)
    to_y_diagonal = remote(outgoing.at[0], landed.at[4], sends.at[4], recvs.at[4], (r, gy))
    to_y_diagonal.start()
    core[1].wait_recv()
    outgoing[1] = (window[slot_of(at_y, here)].astype(wide) + landed[1].astype(wide)).astype(low)
    to_y = remote(outgoing.at[1], landed.at[5], sends.at[5], recvs.at[5], (r, gy))
    to_y.start()
    core[2].wait_recv()
    to_y_diagonal.wait_recv()
    outgoing[2] = (
        window[slot_of(at_x, here)].astype(wide) + landed[2].astype(wide) + landed[4].astype(wide)
    ).astype(low)
    to_x = remote(outgoing.at[2], landed.at[6], sends.at[6], recvs.at[6], (rx, g))
    to_x.start()
    total[...] = window[8].astype(wide)
    sums[...] = window[0].astype(wide)
    core[3].wait_recv()
    blend(c, 0)
    to_y.wait_recv()
    blend(y, 5)
    to_x.wait_recv()
    blend(x, 6)
    outgoing[3] = sums[...].astype(low)
    to_behind = remote(outgoing.at[3], landed.at[7], sends.at[7], recvs.at[7], behind)
    to_behind.start()
    to_behind.wait_recv()
    total[...] += landed[7].astype(wide)
    for copy in core + [to_y_diagonal, to_y, to_x, to_behind]:
        copy.wait_send()


def return_window(window):
    block = window.shape[1:]
    vmem = pl.BlockSpec(memory_space=pltpu.VMEM)
    return pl.pallas_call(
        return_kernel,
        out_shape=jax.ShapeDtypeStruct(block, jnp.float32),
        in_specs=[vmem],
        out_specs=vmem,
        scratch_shapes=[
            pltpu.VMEM((4,) + block, window.dtype),
            pltpu.VMEM((8,) + block, window.dtype),
            pltpu.VMEM(block, jnp.float32),
            pltpu.SemaphoreType.DMA((8,)),
            pltpu.SemaphoreType.DMA((8,)),
        ],
        compiler_params=pltpu.CompilerParams(
            collective_id=3, has_side_effects=True, vmem_limit_bytes=VMEM_LIMIT
        ),
    )(window)


TILES = 8


class Reduction:
    def __init__(self, replicas, chunks, buffers, sends, recvs):
        (
            self.parts,
            self.from_core,
            self.from_y,
            self.from_x,
            self.from_z,
            self.from_far,
            self.final,
        ) = buffers
        self.sends, self.recvs = sends, recvs
        r = lax.axis_index("replica")
        g = lax.axis_index("group")
        self.c, self.y, self.x = lax.rem(g, 2), lax.div(g, 2), lax.rem(r, 2)
        self.z = lax.rem(lax.div(r, 2), 4)
        base = r - 2 * self.z
        self.core_partner = (r, flip_bit(g, 1))
        self.y_partner = (r, flip_bit(g, 2))
        self.x_partner = (flip_bit(r, 1), g)
        self.z_partners = [(base + 2 * lax.rem(self.z + d, 4), g) for d in (1, 2, 3)]
        self.far_partners = []
        bit = 8
        while bit < replicas:
            self.far_partners.append((flip_bit(r, bit), g))
            bit *= 2
        self.pending = []
        self.stages = (
            self.stage_core,
            self.stage_y,
            self.stage_x,
            self.stage_z,
            self.stage_back,
            self.stage_back_x,
            self.stage_end,
        )
        self.state = [None] * chunks

    def greet(self):
        greet(
            [self.core_partner, self.y_partner, self.x_partner] + self.z_partners + self.far_partners
        )

    def advance(self, chunk, stage):
        self.state[chunk] = self.stages[stage](chunk, self.state[chunk])

    def start(self, chunk, slot, source, target, partner):
        copy = remote(source, target, self.sends.at[chunk, slot], self.recvs.at[chunk, slot], partner)
        copy.start()
        self.pending.append(copy)
        return copy

    def finish(self):
        for copy in self.pending:
            copy.wait_send()

    def stage_core(self, k, arrived):
        return self.start(
            k, 0, self.parts.at[1 - self.c, :, k], self.from_core.at[k], self.core_partner
        )

    def stage_y(self, k, arrived):
        arrived.wait_recv()
        parts, c = self.parts, self.c

        def add(t, carry):
            for yy in range(2):
                parts[c, yy, k, t] = (
                    parts[c, yy, k, t].astype(jnp.float32)
                    + self.from_core[k, yy, t].astype(jnp.float32)
                ).astype(jnp.bfloat16)
            return carry

        lax.fori_loop(0, TILES, add, 0)
        return self.start(k, 1, parts.at[c, 1 - self.y, k], self.from_y.at[k], self.y_partner)

    def stage_x(self, k, arrived):
        arrived.wait_recv()
        parts, c, y, x = self.parts, self.c, self.y, self.x
        half = TILES // 2

        def add(t, carry):
            parts[c, y, k, t] = (
                parts[c, y, k, t].astype(jnp.float32) + self.from_y[k, t].astype(jnp.float32)
            ).astype(jnp.bfloat16)
            return carry

        lax.fori_loop(0, TILES, add, 0)
        return self.start(
            k, 2, parts.at[c, y, k, pl.ds((1 - x) * half, half)], self.from_x.at[k], self.x_partner
        )

    def stage_z(self, k, arrived):
        arrived.wait_recv()
        parts, c, y, x = self.parts, self.c, self.y, self.x
        half = TILES // 2

        def add(t, carry):
            parts[c, y, k, x * half + t] = (
                parts[c, y, k, x * half + t].astype(jnp.float32)
                + self.from_x[k, t].astype(jnp.float32)
            ).astype(jnp.bfloat16)
            return carry

        lax.fori_loop(0, half, add, 0)
        return [
            self.start(
                k,
                2 + d,
                parts.at[c, y, k, x * half + lax.rem(self.z + d, 4)],
                self.from_z.at[k, d - 1],
                self.z_partners[d - 1],
            )
            for d in range(1, 4)
        ]

    def stage_back(self, k, arrived):
        for copy in arrived:
            copy.wait_recv()
        final = self.final
        spot = self.x * (TILES // 2) + self.z
        total = self.parts[self.c, self.y, k, spot].astype(jnp.float32)
        for d in range(3):
            total = total + self.from_z[k, d].astype(jnp.float32)
        for step, partner in enumerate(self.far_partners):
            self.from_far[k, 2 * step] = total.astype(jnp.bfloat16)
            copy = self.start(
                k,
                9 + step,
                self.from_far.at[k, 2 * step],
                self.from_far.at[k, 2 * step + 1],
                partner,
            )
            copy.wait_recv()
            total = total + self.from_far[k, 2 * step + 1].astype(jnp.float32)
        final[k, spot] = total.astype(jnp.bfloat16)
        own = final.at[k, spot]
        return [self.start(k, 5 + d, own, own, self.z_partners[d - 1]) for d in range(1, 4)]

    def stage_back_x(self, k, arrived):
        for copy in arrived:
            copy.wait_recv()
        own = self.final.at[k, pl.ds(self.x * (TILES // 2), TILES // 2)]
        return self.start(k, 9 + len(self.far_partners), own, own, self.x_partner)

    def stage_end(self, k, arrived):
        arrived.wait_recv()


def reduction_scratch(replicas, chunks):
    far = max(replicas.bit_length() - 4, 0)
    tile = (144, 128)
    low = jnp.bfloat16
    return [
        pltpu.VMEM((2, 2, chunks, TILES) + tile, low),
        pltpu.VMEM((chunks, 2, TILES) + tile, low),
        pltpu.VMEM((chunks, TILES) + tile, low),
        pltpu.VMEM((chunks, TILES // 2) + tile, low),
        pltpu.VMEM((chunks, 3) + tile, low),
        pltpu.VMEM((chunks, 2 * max(far, 1)) + tile, low),
        pltpu.VMEM((chunks, TILES) + tile, low),
        pltpu.SemaphoreType.DMA((chunks, 10 + far)),
        pltpu.SemaphoreType.DMA((chunks, 10 + far)),
    ]


def put_columns(parts, chunk, tile, product):
    product = product.astype(jnp.bfloat16)
    for s in range(4):
        rows = product[144 * s : 144 * s + 144]
        for j in range(product.shape[1] // 128):
            parts[s % 2, s // 2, chunk, tile + j] = rows[:, j * 128 : j * 128 + 128]


def wide_dot(left, right):
    return jnp.dot(left, right, preferred_element_type=jnp.float32)


FEED_CHUNKS = 5


def feed_kernel(
    replicas,
    normed_two_t,
    attended_t,
    out_grad_t,
    grad_gate,
    grad_up,
    grad_branch,
    hidden,
    bias_t,
    window,
    queries_t,
    grad_attended_t,
    queries_rows,
    grad_attended_rows,
    log_total,
    delta,
    out_gate,
    out_up,
    out_down,
    out_branch,
    grad_window,
    grad_queries_t,
    *scratch,
):
    work = Reduction(replicas, FEED_CHUNKS, scratch[:7], scratch[7], scratch[8])
    parts, final = work.parts, work.final
    work.greet()

    def down_part(chunk, tile, j):
        for s in range(4):
            columns = slice(s * 384 + j * 128, s * 384 + j * 128 + 128)
            product = wide_dot(out_grad_t[...], hidden[:, columns]).astype(jnp.bfloat16)
            for row in range(4):
                parts[s % 2, s // 2, chunk, tile + row] = product[144 * row : 144 * row + 144]

    def columns_part(chunk, tile, left, right, first, last):
        for column in range(first, last, 256):
            put_columns(
                parts,
                chunk,
                tile + (column - first) // 128,
                wide_dot(left[...], right[:, column : column + 256]),
            )

    def products(k):
        if k == 0:
            columns_part(0, 0, normed_two_t, grad_gate, 0, 1024)
        elif k == 1:
            columns_part(1, 0, normed_two_t, grad_gate, 1024, 1536)
            columns_part(1, 4, normed_two_t, grad_up, 0, 512)
        elif k == 2:
            columns_part(2, 0, normed_two_t, grad_up, 512, 1536)
        elif k == 3:
            down_part(3, 0, 0)
            down_part(3, 4, 1)
        else:
            down_part(4, 0, 2)
            columns_part(4, 4, attended_t, grad_branch, 0, 512)

    def write_out(k):
        def columns(target, column, first, count):
            for t in range(count):
                target[:, column + t * 128 : column + t * 128 + 128] = final[k, first + t].astype(
                    jnp.float32
                )

        def rows(first, j):
            block = jnp.concatenate(
                [final[k, first + row].astype(jnp.float32) for row in range(4)], axis=0
            )
            out_down[j * 128 : j * 128 + 128, :] = block.T

        if k == 0:
            columns(out_gate, 0, 0, 8)
        elif k == 1:
            columns(out_gate, 1024, 0, 4)
            columns(out_up, 0, 4, 4)
        elif k == 2:
            columns(out_up, 512, 0, 8)
        elif k == 3:
            rows(0, 0)
            rows(4, 1)
        else:
            rows(0, 2)
            columns(out_branch, 0, 4, 4)

    def attend(c, third):
        lanes = slice(c * 128, c * 128 + 128)
        q_t = queries_t[c]
        a_t = grad_attended_t[c]

        def block(i, carry):
            slot = third * 3 + i
            kv = window[slot, :, lanes]
            bias = bias_t[slot]
            bias = jnp.concatenate([bias, bias, bias], axis=1)
            probs = jnp.exp(wide_dot(kv, q_t) + bias - log_total[c])
            grads = probs * (wide_dot(kv, a_t) - delta[c])
            grads = grads.astype(jnp.bfloat16)
            back = wide_dot(grads, queries_rows[c]) + wide_dot(
                probs.astype(jnp.bfloat16), grad_attended_rows[c]
            )
            grad_window[slot, :, lanes] = back.astype(jnp.bfloat16)
            return carry + contract_rows(kv, grads)

        start = jnp.zeros((128, 768), jnp.float32)
        done = lax.fori_loop(0, 3, block, start)
        if third == 0:
            grad_queries_t[c] = done[:64]
        else:
            grad_queries_t[c] += done[:64]

    last = len(work.stages) - 1
    for t in range(FEED_CHUNKS + last):
        for k in range(FEED_CHUNKS):
            stage = t - k
            if stage == 0:
                products(k)
            if 0 <= stage <= last:
                work.advance(k, stage)
            if stage == last:
                write_out(k)
        if t < 9:
            attend(t // 3, t % 3)
    work.finish()


def feed_and_attention_back(replicas, *operands):
    vmem = pl.BlockSpec(memory_space=pltpu.VMEM)
    wide = jnp.float32
    shapes = [
        jax.ShapeDtypeStruct((144, 1536), wide),
        jax.ShapeDtypeStruct((144, 1536), wide),
        jax.ShapeDtypeStruct((384, 576), wide),
        jax.ShapeDtypeStruct((144, 512), wide),
        jax.ShapeDtypeStruct((9, 256, 384), jnp.bfloat16),
        jax.ShapeDtypeStruct((3, 64, 768), wide),
    ]
    return pl.pallas_call(
        functools.partial(feed_kernel, replicas),
        out_shape=shapes,
        in_specs=[vmem] * len(operands),
        out_specs=[vmem] * len(shapes),
        scratch_shapes=reduction_scratch(replicas, FEED_CHUNKS),
        compiler_params=pltpu.CompilerParams(
            collective_id=4, has_side_effects=True, vmem_limit_bytes=VMEM_LIMIT
        ),
    )(*operands)


def tail_kernel(
    replicas,
    normed_one_t,
    attended_t,
    grad_cols,
    gains,
    out_cols,
    out_gains,
    *scratch,
):
    work = Reduction(replicas, 1, scratch[:7], scratch[7], scratch[8])
    tally, from_gain, gain_sends, gain_recvs = scratch[9:]
    work.greet()
    for pair in range(4):
        right = grad_cols[:, pair * 256 : pair * 256 + 256]
        product = wide_dot(normed_one_t[...], right)
        if pair == 3:
            lane = lax.broadcasted_iota(jnp.int32, product.shape, 1)
            product = jnp.where(lane < 192, product, wide_dot(attended_t[...], right))
        put_columns(work.parts, 0, 2 * pair, product)
    gain_steps = [[work.core_partner], [work.y_partner], [work.x_partner], work.z_partners]
    gain_steps += [[partner] for partner in work.far_partners]
    tally[0] = gains[...]
    flight = []
    slot = 0
    for t in range(max(len(work.stages), len(gain_steps) + 1)):
        if t < len(work.stages):
            work.advance(0, t)
        if flight:
            total = tally[t - 1]
            for copy, landed in flight:
                copy.wait_recv()
                total = total + from_gain[landed]
            flight = []
            if t < len(gain_steps):
                tally[t] = total
            else:
                out_gains[...] = total
        if t < len(gain_steps):
            for partner in gain_steps[t]:
                copy = remote(
                    tally.at[t], from_gain.at[slot], gain_sends.at[slot], gain_recvs.at[slot], partner
                )
                copy.start()
                work.pending.append(copy)
                flight.append((copy, slot))
                slot += 1
    for t in range(TILES):
        out_cols[:, t * 128 : t * 128 + 128] = work.final[0, t].astype(jnp.float32)
    work.finish()


def reduce_tail(replicas, *operands):
    vmem = pl.BlockSpec(memory_space=pltpu.VMEM)
    wide = jnp.float32
    far = max(replicas.bit_length() - 4, 0)
    return pl.pallas_call(
        functools.partial(tail_kernel, replicas),
        out_shape=[
            jax.ShapeDtypeStruct((144, 1024), wide),
            jax.ShapeDtypeStruct((8, 256), wide),
        ],
        in_specs=[vmem] * len(operands),
        out_specs=[vmem] * 2,
        scratch_shapes=reduction_scratch(replicas, 1)
        + [
            pltpu.VMEM((4 + far, 8, 256), wide),
            pltpu.VMEM((6 + far, 8, 256), wide),
            pltpu.SemaphoreType.DMA((6 + far,)),
            pltpu.SemaphoreType.DMA((6 + far,)),
        ],
        compiler_params=pltpu.CompilerParams(
            collective_id=5, has_side_effects=True, vmem_limit_bytes=VMEM_LIMIT
        ),
    )(*operands)


def per_device(
    inputs,
    seg_ids,
    seq_starts,
    gain_one,
    query_w,
    key_w,
    value_weight,
    out_w,
    gain_two,
    gate_w,
    up_w,
    down_w,
    out_grad,
):
    qkvo_all, gate_all, up_all, down_all = gather_weights(
        jnp.concatenate([query_w, key_w, value_weight, out_w], axis=1), gate_w, up_w, down_w
    )
    qkvo_all, gate_all, up_all, down_all = (
        a.reshape(a.shape[0] * a.shape[1], a.shape[2]) for a in (qkvo_all, gate_all, up_all, down_all)
    )
    joined_w = qkvo_all[:, : query_w.shape[1] + 2 * key_w.shape[1]]
    out_all = qkvo_all[:, query_w.shape[1] + 2 * key_w.shape[1] :]
    query_all = qkvo_all[:, : query_w.shape[1]]
    key_all = qkvo_all[:, query_w.shape[1] : query_w.shape[1] + key_w.shape[1]]
    gain_one_all = lax.all_gather(gain_one, "group", axis=0, tiled=True)
    gain_two_all = lax.all_gather(gain_two, "group", axis=0, tiled=True)
    tok_rows = inputs.shape[0]
    query_heads = query_all.shape[1] // HEAD_DIM
    kv_heads = key_all.shape[1] // HEAD_DIM
    repeat_heads = query_heads // kv_heads
    kv_width = kv_heads * HEAD_DIM
    score_scale = 1.0 / math.sqrt(HEAD_DIM)
    reach_back = SEQUENCE_LENGTH // tok_rows
    window_rows = (reach_back + 1) * tok_rows
    device = lax.axis_index(("replica", "group"))
    token_index = device * tok_rows + jnp.arange(tok_rows, dtype=jnp.int32)
    segment_table = jnp.arange(seq_starts.shape[0], dtype=jnp.int32)
    first_token = jnp.sum(
        jnp.where(seg_ids[:, None] == segment_table[None, :], seq_starts[None, :], 0), axis=1
    )
    rotary_angles = rope_angles(token_index - first_token, HEAD_DIM)
    key_index = (device - reach_back) * tok_rows + jnp.arange(window_rows, dtype=jnp.int32)
    visible = (key_index[None, :] <= token_index[:, None]) & (
        key_index[None, :] >= first_token[:, None]
    )
    inputs_wide = inputs.astype(jnp.float32)
    scale_one = rms_scale(inputs_wide)
    gain_one_wide = gain_one_all.astype(jnp.float32)
    first_normed = (inputs_wide * scale_one * gain_one_wide).astype(jnp.bfloat16)
    projected = jnp.dot(first_normed, joined_w, preferred_element_type=jnp.float32)
    query_cols = query_heads * HEAD_DIM
    queries = apply_rotary(
        projected[:, :query_cols].reshape(tok_rows, query_heads, HEAD_DIM), rotary_angles
    ).astype(jnp.bfloat16)
    key_matrix = apply_rotary(
        projected[:, query_cols : query_cols + kv_width].reshape(tok_rows, kv_heads, HEAD_DIM),
        rotary_angles,
    )
    value_matrix = projected[:, query_cols + kv_width :].astype(jnp.bfloat16)
    packed = jnp.concatenate(
        [
            key_matrix.astype(jnp.bfloat16),
            value_matrix.reshape(tok_rows, kv_heads, HEAD_DIM),
        ],
        axis=2,
    ).reshape(tok_rows, 2 * kv_width)
    window_blocks = exchange_window(packed)
    window = window_blocks.reshape(window_rows, kv_heads, 2 * HEAD_DIM)
    key_grid = window[:, :, :HEAD_DIM]
    value_grid = window[:, :, HEAD_DIM:]
    query_grid = queries.reshape(tok_rows, kv_heads, repeat_heads, HEAD_DIM)

    def masked_scores():
        raw_scores = (
            jnp.einsum("tcrd,wcd->crtw", query_grid, key_grid, preferred_element_type=jnp.float32)
            * score_scale
        )
        return jnp.where(visible, raw_scores, masked_score)

    scores = masked_scores()
    row_peak = jnp.max(scores, axis=-1, keepdims=True)
    exponent = jnp.exp(scores - row_peak)
    row_total = jnp.sum(exponent, axis=-1, keepdims=True)
    log_total = row_peak + jnp.log(row_total)
    probs_low = (exponent / row_total).astype(jnp.bfloat16)
    attended_wide = jnp.einsum(
        "crtw,wcd->tcrd", probs_low, value_grid, preferred_element_type=jnp.float32
    )
    attended = attended_wide.reshape(tok_rows, query_cols).astype(jnp.bfloat16)
    middle = inputs_wide + jnp.dot(attended, out_all, preferred_element_type=jnp.float32)
    scale_two = rms_scale(middle)
    gain_two_wide = gain_two_all.astype(jnp.float32)
    normed_two = (middle * scale_two * gain_two_wide).astype(jnp.bfloat16)
    gate = jnp.dot(normed_two, gate_all, preferred_element_type=jnp.float32)
    upper = jnp.dot(normed_two, up_all, preferred_element_type=jnp.float32)
    sigmoid_gate = jax.nn.sigmoid(gate)
    hidden = (gate * sigmoid_gate * upper).astype(jnp.bfloat16)
    outputs = middle + jnp.dot(hidden, down_all, preferred_element_type=jnp.float32)
    grad_hidden = times_transpose(out_grad, down_all)
    grad_gate = (grad_hidden * upper * sigmoid_gate * (1.0 + gate * (1.0 - sigmoid_gate))).astype(
        jnp.bfloat16
    )
    grad_up = (grad_hidden * gate * sigmoid_gate).astype(jnp.bfloat16)
    grad_normed_two = times_transpose(grad_gate, gate_all) + times_transpose(grad_up, up_all)
    grad_middle_norm, grad_gain_two = norm_back(grad_normed_two, middle, scale_two, gain_two_wide)
    grad_middle = out_grad.astype(jnp.float32) + grad_middle_norm
    grad_branch = grad_middle.astype(jnp.bfloat16)
    grad_attended = (
        times_transpose(grad_branch, out_all)
        .astype(jnp.bfloat16)
        .reshape(tok_rows, kv_heads, repeat_heads, HEAD_DIM)
    )
    delta = jnp.sum(grad_attended.astype(jnp.float32) * attended_wide, axis=-1)
    delta = delta.transpose(1, 2, 0).reshape(kv_heads, 1, repeat_heads * tok_rows)
    bias = jnp.where(
        (key_index[:, None] <= token_index[None, :]) & (key_index[:, None] >= first_token[None, :]),
        0.0,
        masked_score,
    ).reshape(reach_back + 1, tok_rows, tok_rows)
    query_rows = (query_grid * jnp.bfloat16(score_scale)).transpose(1, 2, 0, 3)
    query_rows = query_rows.reshape(kv_heads, repeat_heads * tok_rows, HEAD_DIM)
    attended_rows = grad_attended.transpose(1, 2, 0, 3)
    attended_rows = attended_rows.reshape(kv_heads, repeat_heads * tok_rows, HEAD_DIM)
    query_rows = jnp.pad(query_rows, ((0, 0), (0, 0), (0, HEAD_DIM)))
    attended_rows = jnp.pad(attended_rows, ((0, 0), (0, 0), (HEAD_DIM, 0)))
    attended_t = attended.T
    out_gate, out_up, grad_down_w, out_branch, grad_window, grad_query_t = feed_and_attention_back(
        lax.axis_size("replica"),
        normed_two.T,
        attended_t,
        out_grad.T,
        grad_gate,
        grad_up,
        grad_branch,
        hidden,
        bias,
        window_blocks,
        query_rows.transpose(0, 2, 1),
        attended_rows.transpose(0, 2, 1),
        query_rows,
        attended_rows,
        log_total.reshape(kv_heads, 1, repeat_heads * tok_rows),
        delta,
    )
    grad_query_rot = (
        grad_query_t.reshape(kv_heads, HEAD_DIM, repeat_heads, tok_rows).transpose(3, 0, 2, 1)
        * score_scale
    )
    own_grad = return_window(grad_window).reshape(tok_rows, kv_heads, 2 * HEAD_DIM)
    grad_keys = apply_rotary(own_grad[:, :, :HEAD_DIM], -rotary_angles)
    grad_keys = grad_keys.reshape(tok_rows, kv_width).astype(jnp.bfloat16)
    grad_values = own_grad[:, :, HEAD_DIM:].reshape(tok_rows, kv_width).astype(jnp.bfloat16)
    grad_queries = apply_rotary(
        grad_query_rot.reshape(tok_rows, query_heads, HEAD_DIM), -rotary_angles
    )
    grad_queries = grad_queries.reshape(tok_rows, query_cols).astype(jnp.bfloat16)
    grad_qkv = jnp.concatenate([grad_queries, grad_keys, grad_values], axis=1)
    grad_normed_one = times_transpose(grad_qkv, joined_w)
    grad_inputs_norm, grad_gain_one = norm_back(
        grad_normed_one, inputs_wide, scale_one, gain_one_wide
    )
    grad_inputs = grad_middle + grad_inputs_norm
    width = gain_one_all.shape[0]
    gain_grads = jnp.pad(jnp.concatenate([grad_gain_one, grad_gain_two]), (0, 2048 - 2 * width))
    tail, gain_sums = reduce_tail(
        lax.axis_size("replica"),
        first_normed.T,
        attended_t,
        jnp.concatenate([grad_qkv, grad_branch[:, 512:]], axis=1),
        gain_grads.reshape(8, 256),
    )
    gain_sums = gain_sums.reshape(2048)[: 2 * width].reshape(2, width)
    shard = width // lax.axis_size("group")
    gain_sums = lax.dynamic_slice_in_dim(gain_sums, lax.axis_index("group") * shard, shard, 1)
    first = query_cols
    second = first + kv_width
    third = second + kv_width
    return (
        outputs,
        grad_inputs,
        gain_sums[0],
        tail[:, :first],
        tail[:, first:second],
        tail[:, second:third],
        jnp.concatenate([out_branch, tail[:, third:]], axis=1),
        gain_sums[1],
        out_gate,
        out_up,
        grad_down_w,
    )


def solution(mesh):
    placed = (
        P(("replica", "group"), None),
        P(("replica", "group")),
        P(),
        P("group"),
        P("group", None),
        P("group", None),
        P("group", None),
        P("group", None),
        P("group"),
        P("group", None),
        P("group", None),
        P("group", None),
        P(("replica", "group"), None),
    )
    return jax.shard_map(
        per_device,
        mesh=mesh,
        in_specs=placed,
        out_specs=(
            P(("replica", "group"), None),
            P(("replica", "group"), None),
            P("group"),
            P("group", None),
            P("group", None),
            P("group", None),
            P("group", None),
            P("group"),
            P("group", None),
            P("group", None),
            P("group", None),
        ),
        check_vma=False,
    )
```

time: 556 us -> 291 us (0.52)
  blocking collectives: 203 us -> 8.35 us
  waiting for transfers between devices: 191 us -> 0 us
  Pallas kernels: 0 us -> 185 us
  matrix products: 69.2 us -> 29.2 us
  local copies, waits for them, and re-layouts: 17 us -> 52.6 us
  starting transfers between devices: 34.4 us -> 0 us
  between operations: 16.5 us -> 1.91 us
  other arithmetic: 24.3 us -> 12.9 us
    pallas_call x0 -> x5, Pallas kernels: none -> 185 us  [the longest x1 69.4 us: feed_and_attention_back(): pl.pallas_call(functools.partial(feed_kernel, replicas), out_shape=shapes...]
    psum x1 -> x0, blocking collectives: 150 us -> none  [per_device(): lax.psum((owner_sums[0], owner_sums[1], owner_sums[2], owner_sums[3], own...]
    reduce_scatter x6 -> x0, waiting for transfers between devices: 132 us -> none  [the longest x1 31.8 us: per_device(): lax.psum_scatter(grad_up_w.astype(jnp.bfloat16), 'group', scatter_dimensi...]
    dot_general x11 -> x0, matrix products: 42.3 us -> none  [the longest x1 13.2 us: per_device(): jnp.einsum('tcrd,wcd->crtw', grad_attended, value_grid, preferred_element...]
    unnamed x11 -> x0, waiting for transfers between devices: 34.8 us -> none
    ppermute x16 -> x0, starting transfers between devices: 34 us -> none  [from_behind(): return lax.ppermute(block, axis, route)]
    all_gather x4 -> x0, blocking collectives: 32.2 us -> none  [the longest x1 9.06 us: per_device(): lax.all_gather(out_w, 'group', axis=0, tiled=True)]
    ppermute x16 -> x0, waiting for transfers between devices: 24.4 us -> none  [from_behind(): return lax.ppermute(block, axis, route)]
  transfers between devices with their start and end apart: 26 -> 0, of which waited for: 12 -> 0; matrix products, arithmetic and copies ran while one was open for 9% -> 0% of each run, Pallas kernels for 0% -> 0%
where the time goes in v2:
time: 291 us; the launch traced here: 290 us
  Pallas kernels  185 us (64%)
  local copies, waits for them, and re-layouts  52.6 us (18%)
  matrix products  29.2 us (10%)
  other arithmetic  12.9 us (4%)
  blocking collectives  8.35 us (3%)
    pallas_call x1, Pallas kernels, feed_and_attention_back(): pl.pallas_call(functools.partial(feed_kernel, replicas), out_shape=shapes...  69.4 us
    pallas_call x1, Pallas kernels, reduce_tail(): pl.pallas_call(functools.partial(tail_kernel, replicas), out_shape=[jax.S...  34.9 us
    pallas_call x1, Pallas kernels, gather_weights(): pl.pallas_call(gather_kernel, out_shape=[jax.ShapeDtypeStruct((4,) + a.sh...  34.5 us
    unnamed x60, local copies, waits for them, and re-layouts  25.6 us
    pallas_call x1, Pallas kernels, exchange_window(): pl.pallas_call(window_kernel, out_shape=jax.ShapeDtypeStruct((9,) + packe...  24.2 us
    pallas_call x1, Pallas kernels, return_window(): pl.pallas_call(return_kernel, out_shape=jax.ShapeDtypeStruct(block, jnp.f...  22.3 us
    dot_general x1, matrix products, per_device(): jnp.einsum('crtw,wcd->tcrd', probs_low, value_grid, preferred_element_typ...  10.3 us
    unnamed x1, blocking collectives  8.35 us

profile of v2, /device:TPU:0, one launch (start us, length us, event | category | flops | bytes accessed | tf_op | source)
XLA Modules:
  0.0 290.2 jit_solution(3812025722743443360)
XLA Ops:
  0.7 1.3 dynamic-slice
  4.4 8.3 %all-reduce.5 = (bf16[576]{0:T(1024)(128)(2,1)S(1)}, bf16[576]{0:T(1024)(128)(2,1)S(1)}) all-reduce(bf16[576]{0:T(1024)(128)(2,1)S(1)} %dynamic-update-slice, bf16[576]{0:T(1024)(128)(2,1)S(1)} %dynamic-update-slice.1), channel_id=1, replica_groups=mesh['replica'=8,'group'=4] {'group'}, use_global_device_ids=true, to_apply=%add.3 | all-reduce | flops 1152 | bytes 4608
  12.7 1.2 copy.80
  14.0 2.0 copy.81.down
  17.1 34.5 %shard_map.212 = (bf16[4,144,1536]{2,1,0:T(8,128)(2,1)}, bf16[4,144,1536]{2,1,0:T(8,128)(2,1)}, bf16[4,144,1536]{2,1,0:T(8,128)(2,1)}, bf16[4,384,576]{2,1,0:T(8,128)(2,1)}) custom-call(bf16[144,1536]{1,0:T(8,128)(2,1)} %concatenate.39.qkvo, bf16[144,1536]{1,0:T(8,128)(2,1)} %gate.1, bf16[144,1536]{1,0:T(8,128)(2,1)} %up.1, bf16[384,576]{1,0:T(8,128)(2,1)} %copy.81.down), custom_call_target="tpu_custom_call" | custom-call | tf_op jit(solution)/shard_map/pallas_call | solution.py:170
  51.5 2.0 fusion.6
  54.9 24.2 %shard_map.213.window = bf16[9,256,384]{2,1,0:T(8,128)(2,1)} custom-call(bf16[256,384]{1,0:T(8,128)(2,1)} %copy.82.packed), custom_call_target="tpu_custom_call" | custom-call | tf_op jit(solution)/shard_map/pallas_call | solution.py:256
  79.1 4.6 %reshape.309 = bf16[2304,3,128]{2,1,0:T(4,128)(2,1)S(1)} reshape(bf16[9,256,384]{2,1,0:T(8,128)(2,1)} %shard_map.213.window) | data formatting | bytes 3538944 | tf_op jit(solution)/shard_map/reshape | solution.py:837
  83.7 3.5 %fusion.36 = (bf16[2304,3,64]{2,1,0:T(4,128)(2,1)}, bf16[2304,3,64]{2,1,0:T(4,128)(2,1)}) fusion(bf16[2304,3,128]{2,1,0:T(4,128)(2,1)S(1)} %reshape.309), kind=kLoop, calls=%fused_computation.100 | loop fusion | bytes 3538944 | tf_op jit(solution)/shard_map/slice | solution.py:839
  87.3 3.2 %copy.118 = bf16[2304,3,64]{0,2,1:T(8,128)(2,1)S(1)} copy(bf16[2304,3,64]{2,1,0:T(4,128)(2,1)} %get-tuple-element.80) | data formatting | bytes 1769472
  90.6 1.1 compare_and_fusion
  91.7 3.2 %fusion.1 = (f32[3,3,256]{2,1,0:T(4,128)S(1)}, f32[3,2304,256,3]{2,1,3,0:T(8,128)S(1)}) fusion(pred[256,2304]{0,1:T(8,128)(4,1)S(1)} %compare_and_fusion, bf16[256,3,3,32]{0,3,2,1:T(8,128)(2,1)S(1)} %bitcast.112, bf16[256,3,3,32]{0,3,2,1:T(8,128)(2,1)S(1)} %bitcast.110, bf16[2304,3,64]{0,2,1:T(8,128)(2,1)S(1)} %copy.118), kind=kOutput, calls=%fused_computation.4 | convolution fusion | flops 695990016 | bytes 23012352 | tf_op jit(solution)/shard_map/tcrd,wcd->crtw/dot_general | solution.py:844
  95.0 4.5 %fusion = f32[3,3,256]{2,1,0:T(4,128)S(1)} fusion(f32[3,2304,256,3]{2,1,3,0:T(8,128)S(1)} %get-tuple-element.108, f32[3,3,256]{2,1,0:T(4,128)S(1)} %get-tuple-element.107, pred[256,2304]{0,1:T(8,128)(4,1)S(1)} %compare_and_fusion), kind=kLoop, calls=%fused_computation.3 | loop fusion | flops 21231360 | bytes 21841920 | tf_op jit(solution)/shard_map/reduce_sum | solution.py:852
  99.5 3.3 %copy-done = f32[3,2304,256,3]{2,1,3,0:T(8,128)} copy-done((f32[3,2304,256,3]{2,1,3,0:T(8,128)}, f32[3,2304,256,3]{2,1,3,0:T(8,128)S(1)}, u32[]{:S(2)}) %copy-start) | copy-done | bytes 21233688
  102.9 3.0 %copy.117 = bf16[2304,3,64]{0,2,1:T(8,128)(2,1)} copy(bf16[2304,3,64]{2,1,0:T(4,128)(2,1)S(1)} %copy-done.1) | data formatting | bytes 1769472
  105.9 10.3 %fusion.41 = (bf16[256,3,3,64]{0,3,2,1:T(8,128)(2,1)S(1)}, f32[256,3,3,64]{0,3,2,1:T(8,128)S(1)}) fusion(f32[3,2304,256,3]{2,1,3,0:T(8,128)} %copy-done, f32[3,3,256]{2,1,0:T(4,128)S(1)} %fusion, f32[3,3,256]{2,1,0:T(4,128)S(1)} %get-tuple-element.107, pred[256,2304]{0,1:T(8,128)(4,1)S(1)} %compare_and_fusion, bf16[2304,3,64]{0,2,1:T(8,128)(2,1)} %copy.117), kind=kOutput, calls=%fused_computation.105 | convolution fusion | flops 706166784 | bytes 23611392 | tf_op jit(solution)/shard_map/crtw,wcd->tcrd/dot_general | solution.py:855
  116.2 2.0 multiply_reduce_fusion.2
  121.3 2.3 multiply_convert_fusion
  126.6 1.6 convolution_convert_fusion
  131.1 1.5 fusion.38
  132.6 2.1 copy.95.queries_t
  136.8 1.7 and_select_fusion.bias_t
  138.6 69.4 %shard_map.214 = (f32[144,1536]{1,0:T(8,128)}, f32[144,1536]{1,0:T(8,128)}, f32[384,576]{1,0:T(8,128)}, f32[144,512]{1,0:T(8,128)}, bf16[9,256,384]{2,1,0:T(8,128)(2,1)}, /*index=5*/f32[3,64,768]{2,1,0:T(8,128)}) custom-call(bf16[576,256]{1,0:T(8,128)(2,1)} %copy.94.normed_two_t, bf16[576,256]{1,0:T(8,128)(2,1)} %bitcast.102, bf16[576,256]{1,0:T(8,128)(2,1)} %bitcast.100, ...), custom_call_target="tpu_custom_call" | custom-call | tf_op jit(solution)/shard_map/pallas_call | solution.py:680
  209.6 22.3 %shard_map.215 = f32[256,384]{1,0:T(8,128)} custom-call(bf16[9,256,384]{2,1,0:T(8,128)(2,1)} %get-tuple-element.28.window), custom_call_target="tpu_custom_call" | custom-call | tf_op jit(solution)/shard_map/pallas_call | solution.py:339
  231.9 1.2 copy.98
  233.2 2.0 fusion.19
  239.3 34.9 %shard_map.216 = (f32[144,1024]{1,0:T(8,128)}, f32[8,256]{1,0:T(8,128)}) custom-call(bf16[576,256]{1,0:T(8,128)(2,1)} %copy.104.normed_one_t, bf16[576,256]{1,0:T(8,128)(2,1)} %bitcast.103, bf16[256,1024]{1,0:T(8,128)(2,1)} %pad_maximum_fusion.grad_cols, f32[8,256]{1,0:T(8,128)} %reshape.320.gains), custom_call_target="tpu_custom_call" | custom-call | tf_op jit(solution)/shard_map/pallas_call | solution.py:748
  276.0 1.7 slice.96
  277.7 1.9 fusion.37
  281.3 2.4 copy.107
  283.8 2.3 convolution_add_fusion
  287.1 2.1 copy.124
  (111 shorter events, 26.4 us)
Async XLA Ops:
  0.6 15.4 %copy-start.15 = (bf16[144,576]{1,0:T(8,128)(2,1)S(1)}, bf16[144,576]{1,0:T(8,128)(2,1)}, u32[]{:S(2)}) copy-start(bf16[144,576]{1,0:T(8,128)(2,1)} %param.17) | copy-start | bytes 497668
  0.7 15.4 %copy-start.17 = (bf16[144,192]{1,0:T(8,128)(2,1)S(1)}, bf16[144,192]{1,0:T(8,128)(2,1)}, u32[]{:S(2)}) copy-start(bf16[144,192]{1,0:T(8,128)(2,1)} %param.18) | copy-start | bytes 165892
  0.7 15.4 %copy-start.18 = (bf16[144,192]{1,0:T(8,128)(2,1)S(1)}, bf16[144,192]{1,0:T(8,128)(2,1)}, u32[]{:S(2)}) copy-start(bf16[144,192]{1,0:T(8,128)(2,1)} %param.19) | copy-start | bytes 165892
  0.7 15.4 %copy-start.16 = (bf16[144,576]{1,0:T(8,128)(2,1)S(1)}, bf16[144,576]{1,0:T(8,128)(2,1)}, u32[]{:S(2)}) copy-start(bf16[144,576]{1,0:T(8,128)(2,1)} %param.20) | copy-start | bytes 497668
  17.0 36.5 %copy-start.20 = (s32[256]{0:T(256)S(1)}, s32[256]{0:T(256)}, u32[]{:S(2)}) copy-start(s32[256]{0:T(256)} %param.14) | copy-start | bytes 3076
  17.0 36.6 %copy-start.21 = (s32[6]{0:T(128)S(1)}, s32[6]{0:T(128)}, u32[]{:S(2)}) copy-start(s32[6]{0:T(128)} %param.15) | copy-start | bytes 76
  53.6 1.4 copy-start.5
  87.3 3.2 %slice-start = ((f32[256,960]{0,1:T(8,128)}), f32[256,576]{0,1:T(8,128)S(1)}, s32[]{:S(2)}) async-start(f32[256,960]{0,1:T(8,128)} %copy-done.5), calls=%async_computation | async-start | bytes 1179648 | tf_op jit(solution)/shard_map/slice | solution.py:822
  90.6 4.4 %copy-start.13 = (bf16[256,9,32]{0,2,1:T(8,128)(2,1)}, bf16[256,9,32]{0,2,1:T(8,128)(2,1)S(1)}, u32[]{:S(2)}) copy-start(bf16[256,9,32]{0,2,1:T(8,128)(2,1)S(1)} %get-tuple-element.84) | copy-start | bytes 442372
  95.0 7.9 %copy-start = (f32[3,2304,256,3]{2,1,3,0:T(8,128)}, f32[3,2304,256,3]{2,1,3,0:T(8,128)S(1)}, u32[]{:S(2)}) copy-start(f32[3,2304,256,3]{2,1,3,0:T(8,128)S(1)} %get-tuple-element.108) | copy-start | bytes 63700996
  95.0 7.9 %copy-start.1 = (bf16[2304,3,64]{2,1,0:T(4,128)(2,1)S(1)}, bf16[2304,3,64]{2,1,0:T(4,128)(2,1)}, u32[]{:S(2)}) copy-start(bf16[2304,3,64]{2,1,0:T(4,128)(2,1)} %get-tuple-element.79) | copy-start | bytes 2654212
  116.2 2.9 %copy-start.10 = (bf16[256,3,3,64]{0,3,2,1:T(8,128)(2,1)}, bf16[256,3,3,64]{0,3,2,1:T(8,128)(2,1)S(1)}, u32[]{:S(2)}) copy-start(bf16[256,3,3,64]{0,3,2,1:T(8,128)(2,1)S(1)} %get-tuple-element.109) | copy-start | bytes 884740
  116.2 2.0 copy-start.2
  118.3 1.5 copy-start.7
  119.7 1.5 copy-start.6
  119.7 1.6 copy-start.9
  123.6 1.8 copy-start.4
  123.6 1.8 copy-start.12
  125.9 0.7 copy-start.8
  238.4 36.8 %copy-start.14 = (f32[144,512]{1,0:T(8,128)S(1)}, f32[144,512]{1,0:T(8,128)}, u32[]{:S(2)}) copy-start(f32[144,512]{1,0:T(8,128)} %get-tuple-element.31) | copy-start | bytes 884740
  274.2 5.4 %copy-start.19 = (f32[8,256]{1,0:T(8,128)S(1)}, f32[8,256]{1,0:T(8,128)}, u32[]{:S(2)}) copy-start(f32[8,256]{1,0:T(8,128)} %get-tuple-element.29) | copy-start | bytes 24580
  277.7 6.1 %copy-start.3 = (bf16[256,1536]{1,0:T(8,128)(2,1)S(1)}, bf16[256,1536]{1,0:T(8,128)(2,1)}, u32[]{:S(2)}) copy-start(bf16[256,1536]{1,0:T(8,128)(2,1)} %get-tuple-element.78.hidden) | copy-start | bytes 2359300
  286.1 3.2 %copy-start.11 = (f32[144,1536]{1,0:T(8,128)S(1)}, f32[144,1536]{1,0:T(8,128)}, u32[]{:S(2)}) copy-start(f32[144,1536]{1,0:T(8,128)} %get-tuple-element.137) | copy-start | bytes 2654212

commit v3 on v2

--- a/solution.py
+++ b/solution.py
@@ -93,90 +93,94 @@
     )
 
 
-def gather_kernel(qkvo, gate, up, down, qkvo_all, gate_all, up_all, down_all, sends, recvs, local):
-    r = lax.axis_index("replica")
-    g = lax.axis_index("group")
-    core_partner = (r, flip_bit(g, 1))
-    y_partner = (r, flip_bit(g, 2))
-    x_partner = (flip_bit(r, 1), g)
-    x = lax.rem(r, 2)
-    across = flip_bit(g, 2)
-    greet((core_partner, y_partner, x_partner))
-    shards = (qkvo, gate, up, down)
-    wholes = (qkvo_all, gate_all, up_all, down_all)
-
-    def half(whole, owner, part):
-        if whole.shape[2] % 256 == 0:
-            width = whole.shape[2] // 2
-            return whole.at[owner, :, pl.ds(pl.multiple_of(part * width, 128), width)]
-        height = whole.shape[1] // 2
-        return whole.at[owner, pl.ds(pl.multiple_of(part * height, 16), height), :]
-
-    def half_shard(shard, part):
-        if shard.shape[1] % 256 == 0:
-            width = shard.shape[1] // 2
-            return shard.at[:, pl.ds(pl.multiple_of(part * width, 128), width)]
-        height = shard.shape[0] // 2
-        return shard.at[pl.ds(pl.multiple_of(part * height, 16), height), :]
-
-    started = []
-    locals_started = []
-    y_copies = []
-    for i in range(4):
-        copy = remote(
-            half_shard(shards[i], x), half(wholes[i], g, x), sends.at[i, 0], recvs.at[i, 0], y_partner
-        )
+def half_of(shard, part):
+    if shard.shape[-1] % 256 == 0:
+        width = shard.shape[-1] // 2
+        return shard.at[:, pl.ds(pl.multiple_of(part * width, 128), width)]
+    height = shard.shape[-2] // 2
+    return shard.at[pl.ds(pl.multiple_of(part * height, 16), height), :]
+
+
+class Gather:
+    def __init__(self, shards, wholes, sends, recvs, local):
+        self.shards, self.wholes = shards, wholes
+        self.sends, self.recvs, self.local = sends, recvs, local
+        r = lax.axis_index("replica")
+        self.g = lax.axis_index("group")
+        self.x = lax.rem(r, 2)
+        self.core_partner = (r, flip_bit(self.g, 1))
+        self.y_partner = (r, flip_bit(self.g, 2))
+        self.x_partner = (flip_bit(r, 1), self.g)
+        self.across = flip_bit(self.g, 2)
+        self.from_y, self.from_x, self.full, self.own = [], [], [], []
+
+    def start(self, i, slot, source, target, partner):
+        copy = remote(source, target, self.sends.at[i, slot], self.recvs.at[i, slot], partner)
         copy.start()
-        y_copies.append(copy)
-    core_copies = []
-    for i in range(4):
-        copy = remote(
-            shards[i], wholes[i].at[g], sends.at[i, 1], recvs.at[i, 1], core_partner
-        )
-        copy.start()
-        core_copies.append(copy)
-        own = pltpu.make_async_copy(shards[i], wholes[i].at[g], local.at[i])
-        own.start()
-        locals_started.append(own)
-    x_copies = []
-    for i in range(4):
-        y_copies[i].wait_recv()
-        piece = half(wholes[i], across, x)
-        copy = remote(piece, piece, sends.at[i, 2], recvs.at[i, 2], x_partner)
-        copy.start()
-        x_copies.append(copy)
-        copy = remote(piece, piece, sends.at[i, 3], recvs.at[i, 3], core_partner)
-        copy.start()
-        started.append(copy)
-    for i in range(4):
-        x_copies[i].wait_recv()
-        piece = half(wholes[i], across, 1 - x)
-        copy = remote(piece, piece, sends.at[i, 4], recvs.at[i, 4], core_partner)
-        copy.start()
-        started.append(copy)
-    for copy in locals_started:
-        copy.wait()
-    for copy in core_copies:
-        copy.wait()
-    for copy in started:
-        copy.wait()
-    for copy in y_copies + x_copies:
-        copy.wait_send()
-
-
-def gather_weights(qkvo, gate, up, down):
+        return copy
+
+    def begin(self):
+        for i, (shard, whole) in enumerate(zip(self.shards, self.wholes)):
+            self.from_y.append(
+                self.start(
+                    i,
+                    0,
+                    half_of(shard, self.x),
+                    half_of(whole.at[self.g], self.x),
+                    self.y_partner,
+                )
+            )
+        for i, (shard, whole) in enumerate(zip(self.shards, self.wholes)):
+            self.full.append(self.start(i, 1, shard, whole.at[self.g], self.core_partner))
+            own = pltpu.make_async_copy(shard, whole.at[self.g], self.local.at[i])
+            own.start()
+            self.own.append(own)
+
+    def pass_y(self):
+        for i, whole in enumerate(self.wholes):
+            self.from_y[i].wait_recv()
+            piece = half_of(whole.at[self.across], self.x)
+            self.from_x.append(self.start(i, 2, piece, piece, self.x_partner))
+            self.full.append(self.start(i, 3, piece, piece, self.core_partner))
+
+    def pass_x(self):
+        for i, whole in enumerate(self.wholes):
+            self.from_x[i].wait_recv()
+            piece = half_of(whole.at[self.across], 1 - self.x)
+            self.full.append(self.start(i, 4, piece, piece, self.core_partner))
+
+    def finish(self):
+        for copy in self.own + self.full:
+            copy.wait()
+        for copy in self.from_y + self.from_x:
+            copy.wait_send()
+
+
+def gather_kernel(count, *refs):
+    work = Gather(refs[:count], refs[count : 2 * count], *refs[2 * count :])
+    greet((work.core_partner, work.y_partner, work.x_partner))
+    work.begin()
+    work.pass_y()
+    work.pass_x()
+    work.finish()
+
+
+def gather_scratch(count):
+    return [
+        pltpu.SemaphoreType.DMA((count, 5)),
+        pltpu.SemaphoreType.DMA((count, 5)),
+        pltpu.SemaphoreType.DMA((count,)),
+    ]
+
+
+def gather_weights(*arrays):
     vmem = pl.BlockSpec(memory_space=pltpu.VMEM)
-    arrays = (qkvo, gate, up, down)
     return pl.pallas_call(
-        gather_kernel,
+        functools.partial(gather_kernel, len(arrays)),
         out_shape=[jax.ShapeDtypeStruct((4,) + a.shape, a.dtype) for a in arrays],
-        in_specs=[vmem] * 4,
-        out_specs=[vmem] * 4,
-        scratch_shapes=[
-            pltpu.SemaphoreType.DMA((4, 5)),
-            pltpu.SemaphoreType.DMA((4, 5)),
-            pltpu.SemaphoreType.DMA((4,)),
-        ],
+        in_specs=[vmem] * len(arrays),
+        out_specs=[vmem] * len(arrays),
+        scratch_shapes=gather_scratch(len(arrays)),
         compiler_params=pltpu.CompilerParams(
             collective_id=1, has_side_effects=True, vmem_limit_bytes=VMEM_LIMIT
         ),
@@ -195,7 +199,27 @@
     return lax.rem(block - here + 8, 8)
 
 
-def window_kernel(packed, window, sends, recvs, local):
+def forward_kernel(
+    packed,
+    gate,
+    up,
+    down,
+    queries_t,
+    bias_t,
+    window,
+    gate_all,
+    up_all,
+    down_all,
+    attended_t,
+    log_total,
+    peak,
+    sums,
+    mixed,
+    sends,
+    recvs,
+    local,
+    *gather_refs,
+):
     r, g, slabs, slab = place()
     x = lax.rem(r, 2)
     y = lax.div(g, 2)
@@ -204,12 +228,15 @@
     here = x * 4 + g
     at_x, at_y, at_c = (1 - x) * 4 + g, x * 4 + gy, x * 4 + gc
     at_xy = (1 - x) * 4 + gy
+    far_x, far_y = (1 - x) * 4 + gc, x * 4 + flip_bit(gc, 2)
+    far_xy = (1 - x) * 4 + flip_bit(gc, 2)
     ahead = (2 * lax.rem(slab + 1, slabs) + x, g)
     behind = (2 * lax.rem(slab + slabs - 1, slabs) + x, g)
     barrier = pltpu.get_barrier_semaphore()
     for partner in ((rx, g), (r, gy), (r, gc), behind):
         pl.semaphore_signal(barrier, inc=1, device_id=partner, device_id_type=MESH)
     pl.semaphore_wait(barrier, 4)
+    weights = Gather((gate, up, down), (gate_all, up_all, down_all), *gather_refs)
     to_ahead = remote(packed, window.at[0], sends.at[0], recvs.at[0], ahead)
     to_ahead.start()
     firsts = []
@@ -224,9 +251,35 @@
         pl.when(bit == 0)(early.start)
     own = pltpu.make_async_copy(packed, window.at[8], local)
     own.start()
+    weights.begin()
+
+    def attend(slot, first=False):
+        for head in range(3):
+            kv = window[slot, :, head * 128 : head * 128 + 128]
+            bias = bias_t[slot]
+            scores = wide_dot(kv, queries_t[head]) + jnp.concatenate([bias, bias, bias], axis=1)
+            top = jnp.max(scores, axis=0, keepdims=True)
+            if not first:
+                before = peak[head]
+                top = jnp.maximum(before, top)
+                fade = jnp.exp(before - top)
+            exponent = jnp.exp(scores - top)
+            part = jnp.sum(exponent, axis=0, keepdims=True)
+            block = contract_rows(kv, exponent.astype(jnp.bfloat16))
+            peak[head] = top
+            if first:
+                sums[head] = part
+                mixed[head] = block
+            else:
+                sums[head] = sums[head] * fade + part
+                mixed[head] = mixed[head] * fade + block
+
+    own.wait()
+    attend(8, True)
     to_ahead.wait_recv()
     for bit, early, late in firsts:
         pl.when(bit == 1)(late.start)
+    attend(0)
     firsts[0][1].wait_recv()
     slot_x = window.at[slot_of(at_x, here)]
     diagonal = remote(
@@ -239,34 +292,61 @@
     slot_y = window.at[slot_of(at_y, here)]
     core_y = remote(slot_y, window.at[slot_of(at_y, at_c)], sends.at[6], recvs.at[6], (r, gc))
     core_y.start()
+    attend(slot_of(at_x, here))
+    weights.pass_y()
+    attend(slot_of(at_y, here))
     diagonal.wait_recv()
     slot_xy = window.at[slot_of(at_xy, here)]
     core_xy = remote(slot_xy, window.at[slot_of(at_xy, at_c)], sends.at[7], recvs.at[7], (r, gc))
     core_xy.start()
+    attend(slot_of(at_xy, here))
     firsts[2][1].wait_recv()
-    for copy in (core_x, core_y, core_xy):
-        copy.wait_recv()
-    own.wait()
+    attend(slot_of(at_c, here))
+    core_x.wait_recv()
+    attend(slot_of(far_x, here))
+    weights.pass_x()
+    core_y.wait_recv()
+    attend(slot_of(far_y, here))
+    core_xy.wait_recv()
+    attend(slot_of(far_xy, here))
+    for head in range(3):
+        out = mixed[head][64:] / sums[head]
+        for row in range(3):
+            spot = (head * 3 + row) * 64
+            attended_t[spot : spot + 64, :] = out[:, row * 256 : row * 256 + 256]
+        log_total[head] = peak[head] + jnp.log(sums[head])
+    weights.finish()
     for copy in (to_ahead, firsts[0][1], firsts[1][1], firsts[2][1], diagonal, core_x, core_y, core_xy):
         copy.wait_send()
 
 
-def exchange_window(packed):
+def forward_attention(packed, gate, up, down, queries_t, bias_t):
     vmem = pl.BlockSpec(memory_space=pltpu.VMEM)
+    wide = jnp.float32
+    shapes = [jax.ShapeDtypeStruct((9,) + packed.shape, packed.dtype)]
+    shapes += [jax.ShapeDtypeStruct((4,) + a.shape, a.dtype) for a in (gate, up, down)]
+    shapes += [
+        jax.ShapeDtypeStruct((576, 256), wide),
+        jax.ShapeDtypeStruct((3, 1, 768), wide),
+    ]
     return pl.pallas_call(
-        window_kernel,
-        out_shape=jax.ShapeDtypeStruct((9,) + packed.shape, packed.dtype),
-        in_specs=[vmem],
-        out_specs=vmem,
+        forward_kernel,
+        out_shape=shapes,
+        in_specs=[vmem] * 6,
+        out_specs=[vmem] * len(shapes),
         scratch_shapes=[
+            pltpu.VMEM((3, 1, 768), wide),
+            pltpu.VMEM((3, 1, 768), wide),
+            pltpu.VMEM((3, 128, 768), wide),
             pltpu.SemaphoreType.DMA((8,)),
             pltpu.SemaphoreType.DMA((8,)),
             pltpu.SemaphoreType.DMA,
-        ],
+        ]
+        + gather_scratch(3),
         compiler_params=pltpu.CompilerParams(
             collective_id=2, has_side_effects=True, vmem_limit_bytes=VMEM_LIMIT
         ),
-    )(packed)
+    )(packed, gate, up, down, queries_t, bias_t)
 
 
 def return_kernel(window, total, outgoing, landed, sums, sends, recvs):
@@ -781,18 +861,18 @@
     down_w,
     out_grad,
 ):
-    qkvo_all, gate_all, up_all, down_all = gather_weights(
-        jnp.concatenate([query_w, key_w, value_weight, out_w], axis=1), gate_w, up_w, down_w
-    )
-    qkvo_all, gate_all, up_all, down_all = (
-        a.reshape(a.shape[0] * a.shape[1], a.shape[2]) for a in (qkvo_all, gate_all, up_all, down_all)
-    )
+    gains = jnp.stack([gain_one, gain_two])
+    gains = jnp.pad(gains, ((0, 14), (0, 256 - gains.shape[1])))
+    qkvo_all, gains_all = gather_weights(
+        jnp.concatenate([query_w, key_w, value_weight, out_w], axis=1), gains
+    )
+    qkvo_all = qkvo_all.reshape(4 * query_w.shape[0], qkvo_all.shape[2])
+    gain_one_all = gains_all[:, 0, : gain_one.shape[0]].reshape(4 * gain_one.shape[0])
+    gain_two_all = gains_all[:, 1, : gain_one.shape[0]].reshape(4 * gain_one.shape[0])
     joined_w = qkvo_all[:, : query_w.shape[1] + 2 * key_w.shape[1]]
     out_all = qkvo_all[:, query_w.shape[1] + 2 * key_w.shape[1] :]
     query_all = qkvo_all[:, : query_w.shape[1]]
     key_all = qkvo_all[:, query_w.shape[1] : query_w.shape[1] + key_w.shape[1]]
-    gain_one_all = lax.all_gather(gain_one, "group", axis=0, tiled=True)
-    gain_two_all = lax.all_gather(gain_two, "group", axis=0, tiled=True)
     tok_rows = inputs.shape[0]
     query_heads = query_all.shape[1] // HEAD_DIM
     kv_heads = key_all.shape[1] // HEAD_DIM
@@ -809,9 +889,6 @@
     )
     rotary_angles = rope_angles(token_index - first_token, HEAD_DIM)
     key_index = (device - reach_back) * tok_rows + jnp.arange(window_rows, dtype=jnp.int32)
-    visible = (key_index[None, :] <= token_index[:, None]) & (
-        key_index[None, :] >= first_token[:, None]
-    )
     inputs_wide = inputs.astype(jnp.float32)
     scale_one = rms_scale(inputs_wide)
     gain_one_wide = gain_one_all.astype(jnp.float32)
@@ -833,30 +910,27 @@
         ],
         axis=2,
     ).reshape(tok_rows, 2 * kv_width)
-    window_blocks = exchange_window(packed)
-    window = window_blocks.reshape(window_rows, kv_heads, 2 * HEAD_DIM)
-    key_grid = window[:, :, :HEAD_DIM]
-    value_grid = window[:, :, HEAD_DIM:]
-    query_grid = queries.reshape(tok_rows, kv_heads, repeat_heads, HEAD_DIM)
-
-    def masked_scores():
-        raw_scores = (
-            jnp.einsum("tcrd,wcd->crtw", query_grid, key_grid, preferred_element_type=jnp.float32)
-            * score_scale
-        )
-        return jnp.where(visible, raw_scores, masked_score)
-
-    scores = masked_scores()
-    row_peak = jnp.max(scores, axis=-1, keepdims=True)
-    exponent = jnp.exp(scores - row_peak)
-    row_total = jnp.sum(exponent, axis=-1, keepdims=True)
-    log_total = row_peak + jnp.log(row_total)
-    probs_low = (exponent / row_total).astype(jnp.bfloat16)
-    attended_wide = jnp.einsum(
-        "crtw,wcd->tcrd", probs_low, value_grid, preferred_element_type=jnp.float32
-    )
-    attended = attended_wide.reshape(tok_rows, query_cols).astype(jnp.bfloat16)
-    middle = inputs_wide + jnp.dot(attended, out_all, preferred_element_type=jnp.float32)
+    bias = jnp.where(
+        (key_index[:, None] <= token_index[None, :]) & (key_index[:, None] >= first_token[None, :]),
+        0.0,
+        masked_score,
+    ).reshape(reach_back + 1, tok_rows, tok_rows)
+    query_rows = (queries * jnp.bfloat16(score_scale)).reshape(
+        tok_rows, kv_heads, repeat_heads, HEAD_DIM
+    )
+    query_rows = query_rows.transpose(1, 2, 0, 3)
+    query_rows = query_rows.reshape(kv_heads, repeat_heads * tok_rows, HEAD_DIM)
+    query_rows = jnp.pad(query_rows, ((0, 0), (0, 0), (0, HEAD_DIM)))
+    queries_t = query_rows.transpose(0, 2, 1)
+    window_blocks, gate_all, up_all, down_all, attended_t, log_total = forward_attention(
+        packed, gate_w, up_w, down_w, queries_t, bias
+    )
+    gate_all, up_all, down_all = (
+        a.reshape(a.shape[0] * a.shape[1], a.shape[2]) for a in (gate_all, up_all, down_all)
+    )
+    attended_wide = attended_t
+    attended_t = attended_t.astype(jnp.bfloat16)
+    middle = inputs_wide + contract_rows(attended_t, out_all)
     scale_two = rms_scale(middle)
     gain_two_wide = gain_two_all.astype(jnp.float32)
     normed_two = (middle * scale_two * gain_two_wide).astype(jnp.bfloat16)
@@ -874,25 +948,16 @@
     grad_middle_norm, grad_gain_two = norm_back(grad_normed_two, middle, scale_two, gain_two_wide)
     grad_middle = out_grad.astype(jnp.float32) + grad_middle_norm
     grad_branch = grad_middle.astype(jnp.bfloat16)
-    grad_attended = (
-        times_transpose(grad_branch, out_all)
-        .astype(jnp.bfloat16)
-        .reshape(tok_rows, kv_heads, repeat_heads, HEAD_DIM)
-    )
-    delta = jnp.sum(grad_attended.astype(jnp.float32) * attended_wide, axis=-1)
-    delta = delta.transpose(1, 2, 0).reshape(kv_heads, 1, repeat_heads * tok_rows)
-    bias = jnp.where(
-        (key_index[:, None] <= token_index[None, :]) & (key_index[:, None] >= first_token[None, :]),
-        0.0,
-        masked_score,
-    ).reshape(reach_back + 1, tok_rows, tok_rows)
-    query_rows = (query_grid * jnp.bfloat16(score_scale)).transpose(1, 2, 0, 3)
-    query_rows = query_rows.reshape(kv_heads, repeat_heads * tok_rows, HEAD_DIM)
-    attended_rows = grad_attended.transpose(1, 2, 0, 3)
-    attended_rows = attended_rows.reshape(kv_heads, repeat_heads * tok_rows, HEAD_DIM)
-    query_rows = jnp.pad(query_rows, ((0, 0), (0, 0), (0, HEAD_DIM)))
-    attended_rows = jnp.pad(attended_rows, ((0, 0), (0, 0), (HEAD_DIM, 0)))
-    attended_t = attended.T
+    grad_attended_t = times_transpose(out_all, grad_branch).astype(jnp.bfloat16)
+    delta = jnp.sum(
+        (grad_attended_t.astype(jnp.float32) * attended_wide).reshape(
+            query_heads, HEAD_DIM, tok_rows
+        ),
+        axis=1,
+    ).reshape(kv_heads, 1, repeat_heads * tok_rows)
+    back_t = grad_attended_t.reshape(kv_heads, repeat_heads, HEAD_DIM, tok_rows)
+    back_t = back_t.transpose(0, 2, 1, 3).reshape(kv_heads, HEAD_DIM, repeat_heads * tok_rows)
+    back_t = jnp.pad(back_t, ((0, 0), (HEAD_DIM, 0), (0, 0)))
     out_gate, out_up, grad_down_w, out_branch, grad_window, grad_query_t = feed_and_attention_back(
         lax.axis_size("replica"),
         normed_two.T,
@@ -904,11 +969,11 @@
         hidden,
         bias,
         window_blocks,
-        query_rows.transpose(0, 2, 1),
-        attended_rows.transpose(0, 2, 1),
+        queries_t,
+        back_t,
         query_rows,
-        attended_rows,
-        log_total.reshape(kv_heads, 1, repeat_heads * tok_rows),
+        back_t.transpose(0, 2, 1),
+        log_total,
         delta,
     )
     grad_query_rot = (

time: 291 us -> 266 us (0.914); the launches traced: 290 us -> 261 us
  local copies, waits for them, and re-layouts: 52.6 us -> 33.9 us
  Pallas kernels: 185 us -> 197 us
  matrix products: 29.2 us -> 18 us
  blocking collectives: 8.35 us -> 0 us
    dot_general x3 -> x1, matrix products: 15.5 us -> 2.14 us  [contract_rows(): lax.dot_general(former, latter, (((0,), (0,)), ((), ())), preferred_eleme...]
    unnamed x60 -> x54, local copies, waits for them, and re-layouts: 25.6 us -> 13.4 us
    pallas_call x2, Pallas kernels: 58.6 us -> 68.1 us  [the longest x1 48.9 us: forward_attention(): pl.pallas_call(forward_kernel, out_shape=shapes, in_specs=[vmem] * 6, out...]
    unnamed x1 -> x0, blocking collectives: 8.35 us -> none
    reduce_sum x2 -> x1, other arithmetic: 4.62 us -> 0.05 us  [per_device(): jnp.sum((grad_attended_t.astype(jnp.float32) * attended_wide).reshape(que...]
    reshape x2, local copies, waits for them, and re-layouts: 5.22 us -> 0.93 us  [the longest x1 0.61 us: per_device(): delta = jnp.sum((grad_attended_t.astype(jnp.float32) * attended_wide).res...]
    slice x1 -> x0, local copies, waits for them, and re-layouts: 3.55 us -> none  [per_device(): value_grid = window[:, :, HEAD_DIM:]]
    pallas_call x1, Pallas kernels: 22.3 us -> 25.7 us  [return_window(): pl.pallas_call(return_kernel, out_shape=jax.ShapeDtypeStruct(block, jnp.f...]
where the time goes in v3:
time: 266 us; the launch traced here: 261 us
  Pallas kernels  197 us (74%)
  local copies, waits for them, and re-layouts  33.9 us (13%)
  matrix products  18 us (7%)
  other arithmetic  10.9 us (4%)
    pallas_call x1, Pallas kernels, feed_and_attention_back(): pl.pallas_call(functools.partial(feed_kernel, replicas), out_shape=shapes...  69.6 us
    pallas_call x1, Pallas kernels, forward_attention(): pl.pallas_call(forward_kernel, out_shape=shapes, in_specs=[vmem] * 6, out...  48.9 us
    pallas_call x1, Pallas kernels, reduce_tail(): pl.pallas_call(functools.partial(tail_kernel, replicas), out_shape=[jax.S...  33.7 us
    pallas_call x1, Pallas kernels, return_window(): pl.pallas_call(return_kernel, out_shape=jax.ShapeDtypeStruct(block, jnp.f...  25.7 us
    pallas_call x1, Pallas kernels, gather_weights(): pl.pallas_call(functools.partial(gather_kernel, len(arrays)), out_shape=[...  19.2 us
    unnamed x54, local copies, waits for them, and re-layouts  13.4 us
    dot_general x5, matrix products, times_transpose(): lax.dot_general(former, latter, (((1,), (1,)), ((), ())), preferred_eleme...  8.88 us

profile of v3, /device:TPU:0, one launch (start us, length us, event | category | flops | bytes accessed | tf_op | source)
XLA Modules:
  0.0 261.5 jit_solution(1810728659410159772)
XLA Ops:
  0.6 2.1 concatenate.39.refs_0_
  4.6 19.2 %shard_map.212 = (bf16[4,144,1536]{2,1,0:T(8,128)(2,1)}, bf16[4,16,256]{2,1,0:T(8,128)(2,1)}) custom-call(bf16[144,1536]{1,0:T(8,128)(2,1)} %concatenate.39.refs_0_, bf16[16,256]{1,0:T(8,128)(2,1)} %fusion.29.refs_1_), custom_call_target="tpu_custom_call" | custom-call | tf_op jit(solution)/shard_map/pallas_call | solution.py:178
  23.8 1.2 copy.78
  26.7 2.1 fusion.2
  30.7 1.0 copy.82.down
  32.9 1.0 fusion.33
  33.9 1.1 copy.83.queries_t
  35.0 1.6 and_select_fusion.bias_t
  36.6 48.9 %shard_map.213 = (bf16[9,256,384]{2,1,0:T(8,128)(2,1)}, bf16[4,144,1536]{2,1,0:T(8,128)(2,1)}, bf16[4,144,1536]{2,1,0:T(8,128)(2,1)}, bf16[4,384,576]{2,1,0:T(8,...) custom-call(bf16[256,384]{1,0:T(8,128)(2,1)} %copy.81.packed, bf16[144,1536]{1,0:T(8,128)(2,1)} %gate.1, ...), custom_call_target="tpu_custom_call" | custom-call | tf_op jit(solution)/shard_map/pallas_call | solution.py:332
  85.5 1.1 convert_element_type.89.attended_t
  86.6 2.1 multiply_reduce_fusion.2
  89.4 2.4 fusion.35
  93.4 2.3 multiply_convert_fusion
  96.6 1.6 convolution_add_fusion
  98.2 2.1 copy.102
  100.3 2.5 fusion.37
  102.9 1.7 multiply_reduce_fusion
  104.6 1.2 copy.86
  105.8 1.4 fusion.31
  108.2 1.6 convert_multiply_fusion.5
  111.2 1.1 pad_bitcast_fusion.grad_attended_rows
  113.0 69.6 %shard_map.214 = (f32[144,1536]{1,0:T(8,128)}, f32[144,1536]{1,0:T(8,128)}, f32[384,576]{1,0:T(8,128)}, f32[144,512]{1,0:T(8,128)}, bf16[9,256,384]{2,1,0:T(8,128)(2,1)}, /*index=5*/f32[3,64,768]{2,1,0:T(8,128)}) custom-call(bf16[576,256]{1,0:T(8,128)(2,1)} %copy.91.normed_two_t, bf16[576,256]{1,0:T(8,128)(2,1)} %copy-done.4, bf16[576,256]{1,0:T(8,128)(2,1)} %bitcast.72, ...), custom_call_target="tpu_custom_call" | custom-call | tf_op jit(solution)/shard_map/pallas_call | solution.py:760
  182.7 25.7 %shard_map.215 = f32[256,384]{1,0:T(8,128)} custom-call(bf16[9,256,384]{2,1,0:T(8,128)(2,1)} %get-tuple-element.36.window), custom_call_target="tpu_custom_call" | custom-call | tf_op jit(solution)/shard_map/pallas_call | solution.py:419
  208.4 1.2 copy.95
  210.3 1.2 copy-done.13
  212.6 1.0 copy.103
  215.8 0.9 pad_maximum_fusion.grad_cols
  217.5 33.7 %shard_map.216 = (f32[144,1024]{1,0:T(8,128)}, f32[8,256]{1,0:T(8,128)}) custom-call(bf16[576,256]{1,0:T(8,128)(2,1)} %copy.101.normed_one_t, bf16[576,256]{1,0:T(8,128)(2,1)} %copy-done.4, bf16[256,1024]{1,0:T(8,128)(2,1)} %pad_maximum_fusion.grad_cols, f32[8,256]{1,0:T(8,128)} %reshape.294.gains), custom_call_target="tpu_custom_call" | custom-call | tf_op jit(solution)/shard_map/pallas_call | solution.py:828
  252.6 1.7 slice.96
  254.4 1.9 fusion.32
  256.2 1.0 slice.99
  258.0 1.2 copy.104
  (100 shorter events, 21.4 us)
Async XLA Ops:
  25.0 3.8 %copy-start.20 = (s32[256]{0:T(256)S(1)}, s32[256]{0:T(256)}, u32[]{:S(2)}) copy-start(s32[256]{0:T(256)} %param.14) | copy-start | bytes 3076
  25.0 3.8 %copy-start.21 = (s32[6]{0:T(128)S(1)}, s32[6]{0:T(128)}, u32[]{:S(2)}) copy-start(s32[6]{0:T(128)} %param.15) | copy-start | bytes 76
  26.7 2.1 copy-start.18
  26.7 4.1 %copy-start.12 = (bf16[384,576]{0,1:T(8,128)(2,1)S(1)}, bf16[384,576]{0,1:T(8,128)(2,1)}, u32[]{:S(2)}) copy-start(bf16[384,576]{0,1:T(8,128)(2,1)} %param.24) | copy-start | bytes 1327108
  86.5 2.8 %copy-start.4 = (bf16[576,256]{1,0:T(8,128)(2,1)}, bf16[576,256]{1,0:T(8,128)(2,1)S(1)}, u32[]{:S(2)}) copy-start(bf16[576,256]{1,0:T(8,128)(2,1)S(1)} %convert_element_type.89.attended_t) | copy-start | bytes 884740
  89.4 2.4 copy-start
  91.8 1.5 copy-start.6
  91.8 1.5 copy-start.7
  95.7 0.9 copy-start.3
  95.7 7.2 %copy-start.2 = (bf16[256,1536]{1,0:T(8,128)(2,1)}, bf16[256,1536]{1,0:T(8,128)(2,1)S(1)}, u32[]{:S(2)}) copy-start(bf16[256,1536]{1,0:T(8,128)(2,1)S(1)} %get-tuple-element.84.grad_up) | copy-start | bytes 2359300
  105.7 2.4 copy-start.5
  107.2 2.6 copy-start.1
  182.6 27.0 %copy-start.15 = (f32[256,32]{0,1:T(8,128)S(1)}, f32[256,32]{0,1:T(8,128)}, u32[]{:S(2)}) copy-start(f32[256,32]{0,1:T(8,128)} %get-tuple-element.103) | copy-start | bytes 98308
  182.6 27.0 %copy-start.16 = (f32[256,32]{0,1:T(8,128)S(1)}, f32[256,32]{0,1:T(8,128)}, u32[]{:S(2)}) copy-start(f32[256,32]{0,1:T(8,128)} %get-tuple-element.105) | copy-start | bytes 98308
  182.7 27.0 %copy-start.11 = (f32[3,64,768]{2,1,0:T(8,128)S(1)}, f32[3,64,768]{2,1,0:T(8,128)}, u32[]{:S(2)}) copy-start(f32[3,64,768]{2,1,0:T(8,128)} %get-tuple-element.35) | copy-start | bytes 1769476
  210.1 1.5 copy-start.13
  210.1 1.5 copy-start.19
  211.5 0.8 copy-start.17
  215.8 41.4 %copy-start.14 = (f32[144,512]{1,0:T(8,128)S(1)}, f32[144,512]{1,0:T(8,128)}, u32[]{:S(2)}) copy-start(f32[144,512]{1,0:T(8,128)} %get-tuple-element.39) | copy-start | bytes 884740
  216.8 41.2 %copy-start.8 = (f32[384,576]{1,0:T(8,128)S(1)}, f32[384,576]{1,0:T(8,128)}, u32[]{:S(2)}) copy-start(f32[384,576]{1,0:T(8,128)} %get-tuple-element.75) | copy-start | bytes 2654212
  254.4 4.8 %copy-start.10 = (f32[144,1536]{1,0:T(8,128)S(1)}, f32[144,1536]{1,0:T(8,128)}, u32[]{:S(2)}) copy-start(f32[144,1536]{1,0:T(8,128)} %get-tuple-element.138) | copy-start | bytes 2654212
  258.0 2.1 copy-start.9

commit v4 on v3

--- a/solution.py
+++ b/solution.py
@@ -136,15 +136,17 @@
             own.start()
             self.own.append(own)
 
-    def pass_y(self):
-        for i, whole in enumerate(self.wholes):
+    def pass_y(self, *chosen):
+        for i in chosen:
+            whole = self.wholes[i]
             self.from_y[i].wait_recv()
             piece = half_of(whole.at[self.across], self.x)
             self.from_x.append(self.start(i, 2, piece, piece, self.x_partner))
             self.full.append(self.start(i, 3, piece, piece, self.core_partner))
 
-    def pass_x(self):
-        for i, whole in enumerate(self.wholes):
+    def pass_x(self, *chosen):
+        for i in chosen:
+            whole = self.wholes[i]
             self.from_x[i].wait_recv()
             piece = half_of(whole.at[self.across], 1 - self.x)
             self.full.append(self.start(i, 4, piece, piece, self.core_partner))
@@ -160,8 +162,8 @@
     work = Gather(refs[:count], refs[count : 2 * count], *refs[2 * count :])
     greet((work.core_partner, work.y_partner, work.x_partner))
     work.begin()
-    work.pass_y()
-    work.pass_x()
+    work.pass_y(*range(count))
+    work.pass_x(*range(count))
     work.finish()
 
 
@@ -293,20 +295,24 @@
     core_y = remote(slot_y, window.at[slot_of(at_y, at_c)], sends.at[6], recvs.at[6], (r, gc))
     core_y.start()
     attend(slot_of(at_x, here))
-    weights.pass_y()
+    weights.pass_y(0)
     attend(slot_of(at_y, here))
+    weights.pass_y(1)
     diagonal.wait_recv()
     slot_xy = window.at[slot_of(at_xy, here)]
     core_xy = remote(slot_xy, window.at[slot_of(at_xy, at_c)], sends.at[7], recvs.at[7], (r, gc))
     core_xy.start()
     attend(slot_of(at_xy, here))
+    weights.pass_y(2)
     firsts[2][1].wait_recv()
     attend(slot_of(at_c, here))
+    weights.pass_x(0)
     core_x.wait_recv()
     attend(slot_of(far_x, here))
-    weights.pass_x()
+    weights.pass_x(1)
     core_y.wait_recv()
     attend(slot_of(far_y, here))
+    weights.pass_x(2)
     core_xy.wait_recv()
     attend(slot_of(far_xy, here))
     for head in range(3):
@@ -741,8 +747,8 @@
                 work.advance(k, stage)
             if stage == last:
                 write_out(k)
-        if t < 9:
-            attend(t // 3, t % 3)
+        if 2 <= t < 11:
+            attend((t - 2) // 3, (t - 2) % 3)
     work.finish()
 
 
@@ -775,7 +781,11 @@
     attended_t,
     grad_cols,
     gains,
-    out_cols,
+    branch,
+    out_query,
+    out_key,
+    out_value,
+    out_branch,
     out_gains,
     *scratch,
 ):
@@ -816,8 +826,14 @@
                 work.pending.append(copy)
                 flight.append((copy, slot))
                 slot += 1
-    for t in range(TILES):
-        out_cols[:, t * 128 : t * 128 + 128] = work.final[0, t].astype(jnp.float32)
+    columns = jnp.concatenate(
+        [work.final[0, t].astype(jnp.float32) for t in range(TILES)], axis=1
+    )
+    out_query[...] = columns[:, :576]
+    out_key[...] = columns[:, 576:768]
+    out_value[...] = columns[:, 768:960]
+    out_branch[:, :512] = branch[...]
+    out_branch[:, 512:] = columns[:, 960:]
     work.finish()
 
 
@@ -828,11 +844,14 @@
     return pl.pallas_call(
         functools.partial(tail_kernel, replicas),
         out_shape=[
-            jax.ShapeDtypeStruct((144, 1024), wide),
+            jax.ShapeDtypeStruct((144, 576), wide),
+            jax.ShapeDtypeStruct((144, 192), wide),
+            jax.ShapeDtypeStruct((144, 192), wide),
+            jax.ShapeDtypeStruct((144, 576), wide),
             jax.ShapeDtypeStruct((8, 256), wide),
         ],
         in_specs=[vmem] * len(operands),
-        out_specs=[vmem] * 2,
+        out_specs=[vmem] * 5,
         scratch_shapes=reduction_scratch(replicas, 1)
         + [
             pltpu.VMEM((4 + far, 8, 256), wide),
@@ -996,27 +1015,25 @@
     grad_inputs = grad_middle + grad_inputs_norm
     width = gain_one_all.shape[0]
     gain_grads = jnp.pad(jnp.concatenate([grad_gain_one, grad_gain_two]), (0, 2048 - 2 * width))
-    tail, gain_sums = reduce_tail(
+    grad_query_w, grad_key_w, grad_value_w, grad_out_w, gain_sums = reduce_tail(
         lax.axis_size("replica"),
         first_normed.T,
         attended_t,
         jnp.concatenate([grad_qkv, grad_branch[:, 512:]], axis=1),
         gain_grads.reshape(8, 256),
+        out_branch,
     )
     gain_sums = gain_sums.reshape(2048)[: 2 * width].reshape(2, width)
     shard = width // lax.axis_size("group")
     gain_sums = lax.dynamic_slice_in_dim(gain_sums, lax.axis_index("group") * shard, shard, 1)
-    first = query_cols
-    second = first + kv_width
-    third = second + kv_width
     return (
         outputs,
         grad_inputs,
         gain_sums[0],
-        tail[:, :first],
-        tail[:, first:second],
-        tail[:, second:third],
-        jnp.concatenate([out_branch, tail[:, third:]], axis=1),
+        grad_query_w,
+        grad_key_w,
+        grad_value_w,
+        grad_out_w,
         gain_sums[1],
         out_gate,
         out_up,

time: 266 us -> 265 us (level)
    slice x3 -> x0, local copies, waits for them, and re-layouts: 4.56 us -> none  [the longest x1 1.86 us: per_device(): tail[:, second:third]]
    pallas_call x1, Pallas kernels: 69.6 us -> 73.7 us  [feed_and_attention_back(): pl.pallas_call(functools.partial(feed_kernel, replicas), out_shape=shapes...]
    pallas_call x1, Pallas kernels: 25.7 us -> 22.6 us  [return_window(): pl.pallas_call(return_kernel, out_shape=jax.ShapeDtypeStruct(block, jnp.f...]
    unnamed x54 -> x64, local copies, waits for them, and re-layouts: 13.4 us -> 16.3 us
    pallas_call x1, Pallas kernels: 33.7 us -> 36.5 us  [reduce_tail(): pl.pallas_call(functools.partial(tail_kernel, replicas), out_shape=[jax.S...]
where the time goes in v4:
time: 265 us; the launch traced here: 261 us
  Pallas kernels  199 us (75%)
  local copies, waits for them, and re-layouts  32.2 us (12%)
  matrix products  18 us (7%)
  other arithmetic  10.1 us (4%)
    pallas_call x1, Pallas kernels, feed_and_attention_back(): pl.pallas_call(functools.partial(feed_kernel, replicas), out_shape=shapes...  73.7 us
    pallas_call x1, Pallas kernels, forward_attention(): pl.pallas_call(forward_kernel, out_shape=shapes, in_specs=[vmem] * 6, out...  47.2 us
    pallas_call x1, Pallas kernels, reduce_tail(): pl.pallas_call(functools.partial(tail_kernel, replicas), out_shape=[jax.S...  36.5 us
    pallas_call x1, Pallas kernels, return_window(): pl.pallas_call(return_kernel, out_shape=jax.ShapeDtypeStruct(block, jnp.f...  22.6 us
    pallas_call x1, Pallas kernels, gather_weights(): pl.pallas_call(functools.partial(gather_kernel, len(arrays)), out_shape=[...  19.2 us
    unnamed x64, local copies, waits for them, and re-layouts  16.3 us
    dot_general x5, matrix products, times_transpose(): lax.dot_general(former, latter, (((1,), (1,)), ((), ())), preferred_eleme...  8.89 us

profile of v4, /device:TPU:0, one launch (start us, length us, event | category | flops | bytes accessed | tf_op | source)
XLA Modules:
  0.0 261.2 jit_solution(2281073767652711947)
XLA Ops:
  0.6 2.1 concatenate.36.refs_0_
  4.6 19.2 %shard_map.212 = (bf16[4,144,1536]{2,1,0:T(8,128)(2,1)}, bf16[4,16,256]{2,1,0:T(8,128)(2,1)}) custom-call(bf16[144,1536]{1,0:T(8,128)(2,1)} %concatenate.36.refs_0_, bf16[16,256]{1,0:T(8,128)(2,1)} %fusion.29.refs_1_), custom_call_target="tpu_custom_call" | custom-call | tf_op jit(solution)/shard_map/pallas_call | solution.py:180
  23.9 1.2 copy.78
  26.7 2.1 fusion.2
  28.9 0.9 fusion.23
  30.7 1.0 copy.82.down
  32.9 1.0 fusion.32
  33.9 1.1 copy.83.queries_t
  35.0 1.7 and_select_fusion.bias_t
  36.6 47.2 %shard_map.213 = (bf16[9,256,384]{2,1,0:T(8,128)(2,1)}, bf16[4,144,1536]{2,1,0:T(8,128)(2,1)}, bf16[4,144,1536]{2,1,0:T(8,128)(2,1)}, bf16[4,384,576]{2,1,0:T(8,...) custom-call(bf16[256,384]{1,0:T(8,128)(2,1)} %copy.81.packed, bf16[144,1536]{1,0:T(8,128)(2,1)} %gate.1, ...), custom_call_target="tpu_custom_call" | custom-call | tf_op jit(solution)/shard_map/pallas_call | solution.py:338
  83.9 1.1 convert_element_type.89.attended_t
  85.0 2.1 multiply_reduce_fusion.2
  87.8 2.4 fusion.34
  91.8 2.3 multiply_convert_fusion
  95.0 1.7 convolution_add_fusion
  96.7 2.1 copy.102
  98.8 2.5 fusion.36
  101.3 1.7 multiply_reduce_fusion
  103.0 1.2 copy.86
  104.2 1.4 fusion.31
  106.6 1.6 convert_multiply_fusion.5
  109.7 1.1 pad_bitcast_fusion.grad_attended_rows
  111.4 73.7 %shard_map.214 = (f32[144,1536]{1,0:T(8,128)}, f32[144,1536]{1,0:T(8,128)}, f32[384,576]{1,0:T(8,128)}, f32[144,512]{1,0:T(8,128)}, bf16[9,256,384]{2,1,0:T(8,128)(2,1)}, /*index=5*/f32[3,64,768]{2,1,0:T(8,128)}) custom-call(bf16[576,256]{1,0:T(8,128)(2,1)} %copy.91.normed_two_t, bf16[576,256]{1,0:T(8,128)(2,1)} %copy-done.4, bf16[576,256]{1,0:T(8,128)(2,1)} %bitcast.72, ...), custom_call_target="tpu_custom_call" | custom-call | tf_op jit(solution)/shard_map/pallas_call | solution.py:766
  185.1 22.6 %shard_map.215 = f32[256,384]{1,0:T(8,128)} custom-call(bf16[9,256,384]{2,1,0:T(8,128)(2,1)} %get-tuple-element.39.window), custom_call_target="tpu_custom_call" | custom-call | tf_op jit(solution)/shard_map/pallas_call | solution.py:425
  207.8 1.2 copy.95
  209.7 1.2 copy-done.15
  212.0 1.0 copy.103
  215.2 0.9 pad_maximum_fusion.grad_cols
  216.8 36.5 %shard_map.216 = (f32[144,576]{1,0:T(8,128)}, f32[144,192]{1,0:T(8,128)}, f32[144,192]{1,0:T(8,128)}, f32[144,576]{1,0:T(8,128)}, f32[8,256]{1,0:T(8,128)}) custom-call(bf16[576,256]{1,0:T(8,128)(2,1)} %copy.101.normed_one_t, bf16[576,256]{1,0:T(8,128)(2,1)} %copy-done.4, bf16[256,1024]{1,0:T(8,128)(2,1)} %pad_maximum_fusion.grad_cols, ...), custom_call_target="tpu_custom_call" | custom-call | tf_op jit(solution)/shard_map/pallas_call | solution.py:844
  254.9 1.2 copy.104
  259.0 0.9 copy.123
  259.9 0.9 copy.124
  (106 shorter events, 20.7 us)
Async XLA Ops:
  25.0 3.8 %copy-start.23 = (s32[256]{0:T(256)S(1)}, s32[256]{0:T(256)}, u32[]{:S(2)}) copy-start(s32[256]{0:T(256)} %param.14) | copy-start | bytes 3076
  25.0 3.8 %copy-start.24 = (s32[6]{0:T(128)S(1)}, s32[6]{0:T(128)}, u32[]{:S(2)}) copy-start(s32[6]{0:T(128)} %param.15) | copy-start | bytes 76
  26.7 2.1 copy-start.21
  26.7 4.1 %copy-start.12 = (bf16[384,576]{0,1:T(8,128)(2,1)S(1)}, bf16[384,576]{0,1:T(8,128)(2,1)}, u32[]{:S(2)}) copy-start(bf16[384,576]{0,1:T(8,128)(2,1)} %param.24) | copy-start | bytes 1327108
  85.0 2.8 %copy-start.4 = (bf16[576,256]{1,0:T(8,128)(2,1)}, bf16[576,256]{1,0:T(8,128)(2,1)S(1)}, u32[]{:S(2)}) copy-start(bf16[576,256]{1,0:T(8,128)(2,1)S(1)} %convert_element_type.89.attended_t) | copy-start | bytes 884740
  87.8 2.4 copy-start
  90.2 1.5 copy-start.6
  90.2 1.5 copy-start.7
  94.1 0.9 copy-start.3
  94.1 7.2 %copy-start.2 = (bf16[256,1536]{1,0:T(8,128)(2,1)}, bf16[256,1536]{1,0:T(8,128)(2,1)S(1)}, u32[]{:S(2)}) copy-start(bf16[256,1536]{1,0:T(8,128)(2,1)S(1)} %get-tuple-element.90.grad_up) | copy-start | bytes 2359300
  104.2 2.4 copy-start.5
  105.6 2.6 copy-start.1
  185.1 23.9 %copy-start.16 = (f32[256,32]{0,1:T(8,128)S(1)}, f32[256,32]{0,1:T(8,128)}, u32[]{:S(2)}) copy-start(f32[256,32]{0,1:T(8,128)} %get-tuple-element.107) | copy-start | bytes 98308
  185.1 23.9 %copy-start.17 = (f32[256,32]{0,1:T(8,128)S(1)}, f32[256,32]{0,1:T(8,128)}, u32[]{:S(2)}) copy-start(f32[256,32]{0,1:T(8,128)} %get-tuple-element.109) | copy-start | bytes 98308
  185.1 23.9 %copy-start.11 = (f32[3,64,768]{2,1,0:T(8,128)S(1)}, f32[3,64,768]{2,1,0:T(8,128)}, u32[]{:S(2)}) copy-start(f32[3,64,768]{2,1,0:T(8,128)} %get-tuple-element.38) | copy-start | bytes 1769476
  209.4 1.5 copy-start.15
  209.4 1.5 copy-start.22
  210.9 0.8 copy-start.20
  214.9 40.1 %copy-start.8 = (f32[384,576]{1,0:T(8,128)S(1)}, f32[384,576]{1,0:T(8,128)}, u32[]{:S(2)}) copy-start(f32[384,576]{1,0:T(8,128)} %get-tuple-element.81) | copy-start | bytes 2654212
  253.4 2.8 %copy-start.14 = (f32[144,576]{1,0:T(8,128)S(1)}, f32[144,576]{1,0:T(8,128)}, u32[]{:S(2)}) copy-start(f32[144,576]{1,0:T(8,128)} %get-tuple-element.137) | copy-start | bytes 995332
  253.4 3.5 %copy-start.19 = (f32[144,192]{1,0:T(8,128)S(1)}, f32[144,192]{1,0:T(8,128)}, u32[]{:S(2)}) copy-start(f32[144,192]{1,0:T(8,128)} %get-tuple-element.138) | copy-start | bytes 331780
  253.4 4.2 %copy-start.18 = (f32[144,192]{1,0:T(8,128)S(1)}, f32[144,192]{1,0:T(8,128)}, u32[]{:S(2)}) copy-start(f32[144,192]{1,0:T(8,128)} %get-tuple-element.139) | copy-start | bytes 331780
  253.4 4.8 %copy-start.13 = (f32[144,576]{1,0:T(8,128)S(1)}, f32[144,576]{1,0:T(8,128)}, u32[]{:S(2)}) copy-start(f32[144,576]{1,0:T(8,128)} %get-tuple-element.140) | copy-start | bytes 995332
  254.9 4.0 %copy-start.10 = (f32[144,1536]{1,0:T(8,128)S(1)}, f32[144,1536]{1,0:T(8,128)}, u32[]{:S(2)}) copy-start(f32[144,1536]{1,0:T(8,128)} %get-tuple-element.142) | copy-start | bytes 2654212
  256.2 3.7 %copy-start.9 = (f32[144,1536]{1,0:T(8,128)S(1)}, f32[144,1536]{1,0:T(8,128)}, u32[]{:S(2)}) copy-start(f32[144,1536]{1,0:T(8,128)} %get-tuple-element.143) | copy-start | bytes 2654212
